TPU v7x, 32 devices: a whole 2x2x4 slice. The times are simulated.
32 devices in a mesh: ctx: 8 (over y, x, core), head: 4 (over z).
Axes of the slice: x: 2, y: 2, z: 4, core: 2. Of those that a mesh axis runs over, the one named last changes fastest.
Arguments:
- query_in: bfloat16 [1024, 1024], P(('ctx', 'head')), may hold values from -20 to 20
- key_in: bfloat16 [1024, 1024], P('ctx', 'head'), may hold values from -20 to 20
- value_in: bfloat16 [1024, 1024], P('ctx', 'head'), may hold values from -6 to 6
- out_saved: bfloat16 [1024, 1024], P(('ctx', 'head')), may hold values from -1.5 to 1.5
- out_grad: bfloat16 [1024, 1024], P(('ctx', 'head')), may hold values from -24 to 24
- span_place: int32 [16], replicated, may hold values from 0 to 15, each once
Outputs:
- grad_query: bfloat16 [1024, 1024], P(('ctx', 'head'))
- grad_key: bfloat16 [1024, 1024], P('ctx', 'head')
- grad_value: bfloat16 [1024, 1024], P('ctx', 'head')
Inputs may be any that keep to these rules, and one draw needn't show every extreme that they name: `span_place`: each block position appears once.
All inputs are finite; a program needn't handle non-finite values.
Results may differ from a plain program's by a relative error of at most 0.0049.
Values may be sent and summed in bfloat16 or wider, within the bound.
A program may use at most 64 MiB of HBM per device.

v0:
```python
import jax
import jax.numpy as jnp
from jax import lax
from jax.sharding import PartitionSpec as P

HEAD_DIM = 128


def positions_of(span_place, first, count, span_len):
    index = first + jnp.arange(count, dtype=jnp.int32)
    span_id = index // span_len
    table = jnp.arange(span_place.shape[0], dtype=jnp.int32)
    place = jnp.sum(jnp.where(span_id[:, None] == table[None, :], span_place[None, :], 0), axis=1)
    return place * span_len + index % span_len


def heads_view(block):
    return block.reshape(block.shape[0], block.shape[1] // HEAD_DIM, HEAD_DIM)


def block_grads(
    query_part, grad_part, lse_part, delta_part, query_pos, key_part, value_part, key_pos
):
    scale = HEAD_DIM ** (-0.5)
    query_heads = heads_view(query_part)
    grad_heads = heads_view(grad_part)
    key_heads = heads_view(key_part)
    value_heads = heads_view(value_part)
    scores = (
        jnp.einsum("rhd,thd->hrt", query_heads, key_heads, preferred_element_type=jnp.float32)
        * scale
    )
    visible = key_pos[None, None, :] <= query_pos[None, :, None]
    probs = jnp.exp(jnp.where(visible, scores - lse_part[:, :, None], -jnp.inf))
    dprobs = jnp.einsum("rhd,thd->hrt", grad_heads, value_heads, preferred_element_type=jnp.float32)
    dscores = (probs * (dprobs - delta_part[:, :, None]) * scale).astype(jnp.bfloat16)
    grad_q = jnp.einsum("hrt,thd->rhd", dscores, key_heads, preferred_element_type=jnp.float32)
    grad_k = jnp.einsum("hrt,rhd->thd", dscores, query_heads, preferred_element_type=jnp.float32)
    grad_v = jnp.einsum(
        "hrt,rhd->thd", probs.astype(jnp.bfloat16), grad_heads, preferred_element_type=jnp.float32
    )
    return (
        grad_q.reshape(query_part.shape),
        grad_k.reshape(key_part.shape),
        grad_v.reshape(key_part.shape),
    )


def body(query_in, key_in, value_in, out_saved, out_grad, span_place):
    cycle_size = lax.axis_size("ctx")
    my_index = lax.axis_index("ctx")
    row_count = key_in.shape[0]
    span_len = row_count // 2
    feature_width = key_in.shape[1]
    group = feature_width // HEAD_DIM
    scale = HEAD_DIM ** (-0.5)
    query_local, grad_local, saved_local = (
        lax.all_to_all(query_in, "head", split_axis=1, concat_axis=0, tiled=True),
        lax.all_to_all(out_grad, "head", split_axis=1, concat_axis=0, tiled=True),
        lax.all_to_all(out_saved, "head", split_axis=1, concat_axis=0, tiled=True),
    )
    products = grad_local.astype(jnp.float32) * saved_local.astype(jnp.float32)
    delta_rows = jnp.sum(products.reshape(row_count, group, HEAD_DIM), axis=2)
    delta_local = delta_rows.T
    my_pos = positions_of(span_place, my_index * row_count, row_count, span_len)
    query_heads = heads_view(query_local)

    def stat_step(carry, piece, start):
        top, total = carry
        key_pos = positions_of(span_place, start, piece.shape[0], span_len)
        scores = (
            jnp.einsum(
                "rhd,thd->hrt", query_heads, heads_view(piece), preferred_element_type=jnp.float32
            )
            * scale
        )
        visible = key_pos[None, None, :] <= my_pos[None, :, None]
        masked = jnp.where(visible, scores, -jnp.inf)
        new_top = jnp.maximum(top, jnp.max(masked, axis=2))
        total = total * jnp.exp(top - new_top) + jnp.sum(
            jnp.exp(masked - new_top[:, :, None]), axis=2
        )
        return (new_top, total)

    start_top = jnp.full((group, row_count), -1e30, jnp.float32)
    start_total = jnp.zeros((group, row_count), jnp.float32)
    zeros_rows = jnp.zeros((row_count, feature_width), jnp.float32)
    key_all, value_all = (
        lax.all_gather(key_in, "ctx", axis=0, tiled=True),
        lax.all_gather(value_in, "ctx", axis=0, tiled=True),
    )
    total_rows = key_all.shape[0]
    block_count = max(cycle_size // 8, 1)
    block_rows = total_rows // block_count
    key_blocks = key_all.reshape(block_count, block_rows, feature_width)
    value_blocks = value_all.reshape(block_count, block_rows, feature_width)
    block_starts = jnp.arange(block_count, dtype=jnp.int32) * block_rows

    def stat_scan(carry, block):
        piece, first = block
        return (stat_step(carry, piece, first), None)

    stats, unused = lax.scan(stat_scan, (start_top, start_total), (key_blocks, block_starts))
    lse_local = stats[0] + jnp.log(stats[1])

    def grad_scan(grad_q, block):
        key_block, value_block, first = block
        key_pos = positions_of(span_place, first, block_rows, span_len)
        part_q, part_k, part_v = block_grads(
            query_local, grad_local, lse_local, delta_local, my_pos, key_block, value_block, key_pos
        )
        return (grad_q + part_q, (part_k, part_v))

    grad_q, partials = lax.scan(grad_scan, zeros_rows, (key_blocks, value_blocks, block_starts))
    stacked_k = partials[0].reshape(cycle_size, row_count, feature_width)
    stacked_v = partials[1].reshape(cycle_size, row_count, feature_width)
    home_k, home_v = (
        lax.all_to_all(stacked_k, "ctx", split_axis=0, concat_axis=0, tiled=True),
        lax.all_to_all(stacked_v, "ctx", split_axis=0, concat_axis=0, tiled=True),
    )
    grad_k = jnp.sum(home_k, axis=0)
    grad_v = jnp.sum(home_v, axis=0)
    grad_query = lax.all_to_all(
        grad_q.astype(jnp.bfloat16), "head", split_axis=0, concat_axis=1, tiled=True
    )
    return (grad_query, grad_k.astype(jnp.bfloat16), grad_v.astype(jnp.bfloat16))


def solution(mesh):
    placed = (
        P(("ctx", "head"), None),
        P("ctx", "head"),
        P("ctx", "head"),
        P(("ctx", "head"), None),
        P(("ctx", "head"), None),
        P(),
    )
    return jax.shard_map(
        body,
        mesh=mesh,
        in_specs=placed,
        out_specs=(P(("ctx", "head"), None), P("ctx", "head"), P("ctx", "head")),
        check_vma=False,
    )
```

profile of v0, /device:TPU:0, one launch (start us, length us, event | category | flops | bytes accessed | tf_op | source)
XLA Modules:
  0.0 98.9 jit_solution(14831872921901819930)
XLA Ops:
  0.6 1.5 %copy.124 = bf16[4,4,8,256]{3,2,0,1:T(8,128)(2,1)} copy(bf16[4,4,8,256]{3,2,1,0:T(8,128)(2,1)} %bitcast.54) | data formatting | bytes 131072 | tf_op jit(solution)/shard_map/all_to_all | solution.py:58
  2.1 6.4 %all-to-all-start = ((bf16[32,4,256]{2,0,1:T(8,128)(2,1)}), bf16[32,4,256]{2,0,1:T(8,128)(2,1)S(1)}, u32[]{:S(2)}, u32[]{:S(2)}) async-start(bf16[32,4,256]{2,0,1:T(8,128)(2,1)} %bitcast.42), calls=%async_computation | async-start | bytes 131072 | tf_op jit(solution)/shard_map/all_to_all | solution.py:58
  8.6 0.6 copy-done.4
  9.6 0.7 copy-done.1
  10.4 0.7 copy-done.2
  11.1 0.6 copy.122
  12.0 0.6 copy.123
  12.8 10.0 %all_gather.7 = bf16[1024,256]{0,1:T(8,128)(2,1)S(1)} all-gather(bf16[128,256]{0,1:T(8,128)(2,1)S(1)} %copy.76), channel_id=1, replica_groups=mesh['ctx'=8,'head'=4] {'ctx'}, dimensions={0}, use_global_device_ids=true | all-gather | bytes 589824 | tf_op jit(solution)/shard_map/all_gather | solution.py:90
  22.7 5.1 %all-to-all-start.2 = ((bf16[32,4,256]{2,0,1:T(8,128)(2,1)}), bf16[32,4,256]{2,0,1:T(8,128)(2,1)S(1)}, u32[]{:S(2)}, u32[]{:S(2)}) async-start(bf16[32,4,256]{2,0,1:T(8,128)(2,1)} %bitcast.40), calls=%async_computation.2 | async-start | bytes 131072 | tf_op jit(solution)/shard_map/all_to_all | solution.py:60
  27.9 9.9 %all_gather.6 = bf16[1024,256]{0,1:T(8,128)(2,1)S(1)} all-gather(bf16[128,256]{0,1:T(8,128)(2,1)S(1)} %copy.72), channel_id=1, replica_groups=mesh['ctx'=8,'head'=4] {'ctx'}, dimensions={0}, use_global_device_ids=true | all-gather | bytes 589824 | tf_op jit(solution)/shard_map/all_gather | solution.py:89
  37.8 5.1 %all-to-all-start.1 = ((bf16[32,4,256]{2,0,1:T(8,128)(2,1)}), bf16[32,4,256]{2,0,1:T(8,128)(2,1)S(1)}, u32[]{:S(2)}, u32[]{:S(2)}) async-start(bf16[32,4,256]{2,0,1:T(8,128)(2,1)} %bitcast.41), calls=%async_computation.1 | async-start | bytes 131072 | tf_op jit(solution)/shard_map/all_to_all | solution.py:59
  43.0 5.6 %all-to-all-done.1 = bf16[32,4,256]{2,0,1:T(8,128)(2,1)S(1)} async-done(((bf16[32,4,256]{2,0,1:T(8,128)(2,1)}), bf16[32,4,256]{2,0,1:T(8,128)(2,1)S(1)}, u32[]{:S(2)}, u32[]{:S(2)}) %all-to-all-start.1) | async-done | bytes 65568 | tf_op jit(solution)/shard_map/all_to_all | solution.py:59
  49.0 0.4 select_reduce_fusion
  49.4 0.3 exponential_reduce_fusion
  49.8 0.5 fusion.2
  50.2 0.3 fusion.3
  50.6 0.7 convert_element_type.45
  51.3 3.3 %all-to-all-start.3 = ((bf16[4,32,256]{2,1,0:T(8,128)(2,1)}), bf16[4,32,256]{2,1,0:T(8,128)(2,1)S(1)}, u32[]{:S(2)}, u32[]{:S(2)}) async-start(bf16[4,32,256]{2,1,0:T(8,128)(2,1)} %convert_element_type.45), calls=%async_computation.3 | async-start | bytes 131072 | tf_op jit(solution)/shard_map/all_to_all | solution.py:123
  54.6 0.5 convolution_bitcast_fusion
  55.1 0.3 copy.91
  55.6 1.2 %copy.92 = f32[8,128,256]{1,2,0:T(8,128)} copy(f32[8,128,256]{1,0,2:T(8,128)S(1)} %bitcast.46) | data formatting | bytes 2097152 | tf_op jit(solution)/shard_map/reshape | solution.py:116
  56.8 3.5 %all-to-all-done.3 = bf16[4,32,256]{2,1,0:T(8,128)(2,1)S(1)} async-done(((bf16[4,32,256]{2,1,0:T(8,128)(2,1)}), bf16[4,32,256]{2,1,0:T(8,128)(2,1)S(1)}, u32[]{:S(2)}, u32[]{:S(2)}) %all-to-all-start.3) | async-done | bytes 65568 | tf_op jit(solution)/shard_map/all_to_all | solution.py:123
  60.3 3.6 %all-to-all-start.5 = ((f32[8,128,256]{1,2,0:T(8,128)}), f32[8,128,256]{1,2,0:T(8,128)S(1)}, u32[]{:S(2)}, u32[]{:S(2)}) async-start(f32[8,128,256]{1,2,0:T(8,128)} %copy.92), calls=%async_computation.5 | async-start | bytes 2097152 | tf_op jit(solution)/shard_map/all_to_all | solution.py:119
  63.9 0.3 convolution_bitcast_fusion.1
  64.2 0.3 copy.86
  64.8 1.2 %copy.87 = f32[8,128,256]{1,2,0:T(8,128)} copy(f32[8,128,256]{1,0,2:T(8,128)S(1)} %bitcast.48) | data formatting | bytes 2097152 | tf_op jit(solution)/shard_map/reshape | solution.py:115
  65.9 13.3 %all-to-all-done.5 = f32[8,128,256]{1,2,0:T(8,128)S(1)} async-done(((f32[8,128,256]{1,2,0:T(8,128)}), f32[8,128,256]{1,2,0:T(8,128)S(1)}, u32[]{:S(2)}, u32[]{:S(2)}) %all-to-all-start.5) | async-done | bytes 1048608 | tf_op jit(solution)/shard_map/all_to_all | solution.py:119
  79.2 3.6 %all-to-all-start.4 = ((f32[8,128,256]{1,2,0:T(8,128)}), f32[8,128,256]{1,2,0:T(8,128)S(1)}, u32[]{:S(2)}, u32[]{:S(2)}) async-start(f32[8,128,256]{1,2,0:T(8,128)} %copy.87), calls=%async_computation.4 | async-start | bytes 2097152 | tf_op jit(solution)/shard_map/all_to_all | solution.py:118
  82.8 0.6 copy.106
  83.5 0.7 copy.95
  84.2 13.9 %all-to-all-done.4 = f32[8,128,256]{1,2,0:T(8,128)S(1)} async-done(((f32[8,128,256]{1,2,0:T(8,128)}), f32[8,128,256]{1,2,0:T(8,128)S(1)}, u32[]{:S(2)}, u32[]{:S(2)}) %all-to-all-start.4) | async-done | bytes 1048608 | tf_op jit(solution)/shard_map/all_to_all | solution.py:118
  98.2 0.7 copy.94
  (31 shorter events, 1.8 us)
Async XLA Ops:
  2.1 7.3 %copy-start = (bf16[128,256]{1,0:T(8,128)(2,1)S(1)}, bf16[128,256]{1,0:T(8,128)(2,1)}, u32[]{:S(2)}) copy-start(bf16[128,256]{1,0:T(8,128)(2,1)} %param.7) | copy-start | bytes 196612
  2.1 20.6 %all-to-all-start = ((bf16[32,4,256]{2,0,1:T(8,128)(2,1)}), bf16[32,4,256]{2,0,1:T(8,128)(2,1)S(1)}, u32[]{:S(2)}, u32[]{:S(2)}) async-start(bf16[32,4,256]{2,0,1:T(8,128)(2,1)} %bitcast.42), calls=%async_computation | async-start | bytes 131072 | tf_op jit(solution)/shard_map/all_to_all | solution.py:58
  8.6 0.7 copy-start.4
  9.4 0.8 copy-start.1
  10.3 0.8 copy-start.2
  11.1 0.9 copy-start.3
  22.7 15.1 %all-to-all-start.2 = ((bf16[32,4,256]{2,0,1:T(8,128)(2,1)}), bf16[32,4,256]{2,0,1:T(8,128)(2,1)S(1)}, u32[]{:S(2)}, u32[]{:S(2)}) async-start(bf16[32,4,256]{2,0,1:T(8,128)(2,1)} %bitcast.40), calls=%async_computation.2 | async-start | bytes 131072 | tf_op jit(solution)/shard_map/all_to_all | solution.py:60
  37.8 10.9 %all-to-all-start.1 = ((bf16[32,4,256]{2,0,1:T(8,128)(2,1)}), bf16[32,4,256]{2,0,1:T(8,128)(2,1)S(1)}, u32[]{:S(2)}, u32[]{:S(2)}) async-start(bf16[32,4,256]{2,0,1:T(8,128)(2,1)} %bitcast.41), calls=%async_computation.1 | async-start | bytes 131072 | tf_op jit(solution)/shard_map/all_to_all | solution.py:59
  51.3 9.0 %all-to-all-start.3 = ((bf16[4,32,256]{2,1,0:T(8,128)(2,1)}), bf16[4,32,256]{2,1,0:T(8,128)(2,1)S(1)}, u32[]{:S(2)}, u32[]{:S(2)}) async-start(bf16[4,32,256]{2,1,0:T(8,128)(2,1)} %convert_element_type.45), calls=%async_computation.3 | async-start | bytes 131072 | tf_op jit(solution)/shard_map/all_to_all | solution.py:123
  60.3 18.9 %all-to-all-start.5 = ((f32[8,128,256]{1,2,0:T(8,128)}), f32[8,128,256]{1,2,0:T(8,128)S(1)}, u32[]{:S(2)}, u32[]{:S(2)}) async-start(f32[8,128,256]{1,2,0:T(8,128)} %copy.92), calls=%async_computation.5 | async-start | bytes 2097152 | tf_op jit(solution)/shard_map/all_to_all | solution.py:119
  79.2 18.9 %all-to-all-start.4 = ((f32[8,128,256]{1,2,0:T(8,128)}), f32[8,128,256]{1,2,0:T(8,128)S(1)}, u32[]{:S(2)}, u32[]{:S(2)}) async-start(f32[8,128,256]{1,2,0:T(8,128)} %copy.87), calls=%async_computation.4 | async-start | bytes 2097152 | tf_op jit(solution)/shard_map/all_to_all | solution.py:118
where the time goes:
time: 99.8 us; the launch traced here: 98.9 us
  waiting for transfers between devices  36.3 us (36%)
  starting transfers between devices  27.1 us (27%)
  blocking collectives  19.9 us (20%)
  local copies, waits for them, and re-layouts  11.8 us (12%)
  matrix products  2.03 us (2%)
  other arithmetic  1.04 us (1%)
    all_to_all x1, waiting for transfers between devices, body(): lax.all_to_all(stacked_k, 'ctx', split_axis=0, concat_axis=0, tiled=True)  13.9 us
    all_to_all x1, waiting for transfers between devices, body(): lax.all_to_all(stacked_v, 'ctx', split_axis=0, concat_axis=0, tiled=True)  13.3 us
    all_gather x1, blocking collectives, body(): lax.all_gather(value_in, 'ctx', axis=0, tiled=True)  9.99 us
    all_gather x1, blocking collectives, body(): lax.all_gather(key_in, 'ctx', axis=0, tiled=True)  9.95 us
    all_to_all x1, starting transfers between devices, body(): lax.all_to_all(query_in, 'head', split_axis=1, concat_axis=0, tiled=True)  6.45 us
    all_to_all x1, waiting for transfers between devices, body(): lax.all_to_all(out_grad, 'head', split_axis=1, concat_axis=0, tiled=True)  5.63 us
    all_to_all x1, starting transfers between devices, body(): lax.all_to_all(out_saved, 'head', split_axis=1, concat_axis=0, tiled=True)  5.11 us
    all_to_all x1, starting transfers between devices, body(): lax.all_to_all(out_grad, 'head', split_axis=1, concat_axis=0, tiled=True)  5.11 us
  transfers between devices with their start and end apart: 6, of which 4 were waited for; matrix products, arithmetic and copies ran while one was open for 8% of the time, Pallas kernels for 0%

commit v1 on v0

v1 whole, which is shorter than its diff:
```python
import functools
import math

import jax
import jax.numpy as jnp
from jax import lax
from jax.experimental import pallas as pl
from jax.experimental.pallas import tpu as pltpu
from jax.sharding import PartitionSpec as P

HEAD_DIM = 128
CORES = 2
MESH = pl.DeviceIdType.MESH
NT = (((1,), (1,)), ((), ()))
NN = (((1,), (0,)), ((), ()))
TN = (((0,), (0,)), ((), ()))


def matmul(a, b, dims):
    return lax.dot_general(a, b, dims, preferred_element_type=jnp.float32)


def columns(index):
    return pl.ds(pl.multiple_of(index * HEAD_DIM, HEAD_DIM), HEAD_DIM)


def kernel(
    ctx_size, head_size, place, query_in, key_in, value_in, saved_in, grad_in,
    dq_out, dk_out, dv_out,
    qbuf, gbuf, dbuf, kbuf, vbuf, pbuf, dk_stage, dv_stage, dq_stage, kpart, vpart, qpart,
    own_grad, own_saved, delta_src,
    send_sem, local_sem, q_sem, g_sem, d_sem, k_sem, v_sem, kp_sem, vp_sem, qp_sem,
):
    chips = ctx_size // CORES
    rows_high = max(chips // 2, 1)
    block = key_in.shape[0]
    token_rows = query_in.shape[0]
    heads = head_size * CORES
    rows = CORES * block
    span = ctx_size * block // place.shape[0]
    spans = rows // span
    scale = HEAD_DIM ** -0.5

    me = lax.axis_index("ctx")
    z = lax.axis_index("head")
    core = lax.rem(me, CORES)
    chip = me // CORES
    low, high = lax.rem(chip, 2), chip // 2

    def other_chip(step):
        return lax.rem(high + step // 2, rows_high) * 2 + lax.rem(low + step % 2, 2)

    def other_core(step):
        return lax.rem(core + step, CORES)

    def other_z(step):
        return lax.rem(z + step, head_size)

    chip_at = [other_chip(step) for step in range(chips)]
    core_at = [other_core(step) for step in range(CORES)]
    z_at = [other_z(step) for step in range(head_size)]
    plane = [(c, j) for c in range(chips) for j in range(CORES) if c or j]
    line = [(w, j) for w in range(head_size) for j in range(CORES) if w or j]

    def plane_id(c, j):
        return {"ctx": chip_at[c] * CORES + core_at[j], "head": z}

    def line_id(w, j):
        return {"ctx": chip * CORES + core_at[j], "head": z_at[w]}

    barrier = pltpu.get_barrier_semaphore()
    peers = [plane_id(c, j) for c, j in plane] + [line_id(w, j) for w, j in line if w]
    for peer in peers:
        pl.semaphore_signal(barrier, inc=1, device_id=peer, device_id_type=MESH)

    grad_load = pltpu.make_async_copy(grad_in, own_grad, local_sem.at[0])
    saved_load = pltpu.make_async_copy(saved_in, own_saved, local_sem.at[1])
    grad_load.start()
    saved_load.start()
    my_head = z * CORES + core
    pltpu.make_async_copy(query_in.at[:, columns(my_head)], qbuf.at[core, z], q_sem.at[core, z]).start()
    pltpu.make_async_copy(key_in.at[:, columns(core)], kbuf.at[chip, core], k_sem.at[chip, core]).start()
    pltpu.make_async_copy(grad_in.at[:, columns(my_head)], gbuf.at[core, z], g_sem.at[core, z]).start()
    pltpu.make_async_copy(value_in.at[:, columns(core)], vbuf.at[chip, core], v_sem.at[chip, core]).start()

    grad_load.wait()
    saved_load.wait()
    product = own_grad[...].astype(jnp.float32) * own_saved[...].astype(jnp.float32)
    coarse = product.astype(jnp.bfloat16)
    fine = (product - coarse.astype(jnp.float32)).astype(jnp.bfloat16)
    shape = (heads, heads * HEAD_DIM)
    member = lax.broadcasted_iota(jnp.int32, shape, 1) // HEAD_DIM == lax.broadcasted_iota(jnp.int32, shape, 0)
    member = jnp.where(member, 1.0, 0.0).astype(jnp.bfloat16)
    delta = matmul(member, jnp.concatenate([coarse] * head_size, axis=0), NT)
    delta += matmul(member, jnp.concatenate([fine] * head_size, axis=0), NT)
    lane_z = lax.broadcasted_iota(jnp.int32, (heads, block), 1) // token_rows
    delta = jnp.where(lane_z == z, delta, 0.0)
    for h in range(heads):
        delta_src[h] = delta[h : h + 1]
    dbuf[core, z] = delta_src[my_head]

    pl.semaphore_wait(barrier, len(peers))

    sent = []

    def send(src, dst, sem, device):
        copy = pltpu.make_async_remote_copy(
            src_ref=src, dst_ref=dst, send_sem=send_sem.at[len(sent)], recv_sem=sem,
            device_id=device, device_id_type=MESH,
        )
        copy.start()
        sent.append(copy)

    def arrive(dst, sem):
        pltpu.make_async_copy(dst, dst, sem).wait()

    def send_plane(src, dst, sem):
        for c, j in plane[::-1]:
            send(src.at[:, columns(core_at[j])], dst.at[chip, core], sem.at[chip, core], plane_id(c, j))

    def send_line(src, dst, sem):
        for w, j in line:
            head = z_at[w] * CORES + core_at[j]
            send(src.at[:, columns(head)], dst.at[core, z], sem.at[core, z], line_id(w, j))

    send_line(query_in, qbuf, q_sem)
    send_plane(key_in, kbuf, k_sem)
    send_line(grad_in, gbuf, g_sem)
    send_plane(value_in, vbuf, v_sem)
    for w, j in line:
        head = z_at[w] * CORES + core_at[j]
        send(delta_src.at[head], dbuf.at[core, z], d_sem.at[core, z], line_id(w, j))

    lane = lax.broadcasted_iota(jnp.int32, (1, rows), 1)
    place_row = jnp.zeros((1, rows), jnp.int32)
    for s in range(spans):
        place_row = jnp.where(lane // span == s, place[chip * spans + s], place_row)
    pos_row = place_row * span + lane % span
    within = lax.broadcasted_iota(jnp.int32, (span, rows), 0)

    for j in range(CORES):
        for w in range(head_size):
            arrive(qbuf.at[j, w], q_sem.at[j, w])
    query = qbuf[...].reshape(rows, HEAD_DIM)

    tops, sums = [], []
    for c in range(chips):
        for j in range(CORES):
            arrive(kbuf.at[chip_at[c], j], k_sem.at[chip_at[c], j])
        keys = kbuf[chip_at[c]].reshape(rows, HEAD_DIM)
        scores = matmul(keys, query, NT) * (scale * math.log2(math.e))
        pieces = []
        for s in range(spans):
            limit = pos_row - place[chip_at[c] * spans + s] * span
            pieces.append(jnp.where(within <= limit, scores[s * span : (s + 1) * span], -1e30))
        masked = jnp.concatenate(pieces, axis=0)
        top = jnp.max(masked, axis=0, keepdims=True)
        probs = jnp.exp2(masked - top)
        pbuf[c] = probs
        tops.append(top)
        sums.append(jnp.sum(probs, axis=0, keepdims=True))

    best = functools.reduce(jnp.maximum, tops)
    weights = [jnp.exp2(top - best) for top in tops]
    total = functools.reduce(jnp.add, [w * s for w, s in zip(weights, sums)])
    weights = [w / total for w in weights]

    for j in range(CORES):
        for w in range(head_size):
            arrive(gbuf.at[j, w], g_sem.at[j, w])
    grad = gbuf[...].reshape(rows, HEAD_DIM)
    for w, j in line:
        arrive(dbuf.at[core_at[j], z_at[w]], d_sem.at[core_at[j], z_at[w]])
    delta_row = jnp.concatenate(
        [functools.reduce(jnp.add, [dbuf[j, w] for w in range(head_size)]) for j in range(CORES)], axis=1
    )

    grad_q = jnp.zeros((rows, HEAD_DIM), jnp.float32)
    for c in range(chips)[::-1]:
        for j in range(CORES):
            arrive(vbuf.at[chip_at[c], j], v_sem.at[chip_at[c], j])
        values = vbuf[chip_at[c]].reshape(rows, HEAD_DIM)
        probs = pbuf[c] * weights[c]
        dv_stage[c] = matmul(probs.astype(jnp.bfloat16), grad, NN).astype(jnp.bfloat16).reshape(dv_stage.shape[1:])
        dprobs = matmul(values, grad, NT)
        dscores = (probs * (dprobs - delta_row) * scale).astype(jnp.bfloat16)
        dk_stage[c] = matmul(dscores, query, NN).astype(jnp.bfloat16).reshape(dk_stage.shape[1:])
        for stage, part, sem in ((dv_stage, vpart, vp_sem), (dk_stage, kpart, kp_sem)):
            for j in range(CORES):
                if c or j:
                    send(stage.at[c, core_at[j]], part.at[chip, core], sem.at[chip, core], plane_id(c, j))
                else:
                    part[chip, core] = stage[c, core]
        grad_q += matmul(dscores, kbuf[chip_at[c]].reshape(rows, HEAD_DIM), TN)

    dq_stage[...] = grad_q.astype(jnp.bfloat16).reshape(dq_stage.shape)
    qpart[my_head] = dq_stage[core, z]
    for w, j in line:
        send(dq_stage.at[core_at[j], z_at[w]], qpart.at[my_head], qp_sem.at[my_head], line_id(w, j))

    for part, sem, out in ((vpart, vp_sem, dv_out), (kpart, kp_sem, dk_out)):
        for c, j in plane:
            arrive(part.at[chip_at[c], core_at[j]], sem.at[chip_at[c], core_at[j]])
        for j in range(CORES):
            summed = part[0, j].astype(jnp.float32)
            for c in range(1, chips):
                summed += part[c, j].astype(jnp.float32)
            out[:, j * HEAD_DIM : (j + 1) * HEAD_DIM] = summed.astype(jnp.bfloat16)

    for w, j in line:
        head = z_at[w] * CORES + core_at[j]
        arrive(qpart.at[head], qp_sem.at[head])
    for h in range(heads):
        dq_out[:, h * HEAD_DIM : (h + 1) * HEAD_DIM] = qpart[h]
    for copy in sent:
        copy.wait_send()


def body(query_in, key_in, value_in, out_saved, out_grad, span_place):
    ctx_size, head_size = lax.axis_size("ctx"), lax.axis_size("head")
    chips = ctx_size // CORES
    block = key_in.shape[0]
    token_rows, width = query_in.shape
    heads = head_size * CORES
    rows = CORES * block
    low = jnp.bfloat16
    tokens = (CORES, head_size, token_rows, HEAD_DIM)
    keys = (chips, CORES, block, HEAD_DIM)
    dma = pltpu.SemaphoreType.DMA
    copies = 4 * (ctx_size - 1) + 4 * (heads - 1)
    vmem = pl.BlockSpec(memory_space=pltpu.VMEM)
    hbm = pl.BlockSpec(memory_space=pl.ANY)
    smem = pl.BlockSpec(memory_space=pltpu.SMEM)
    pairs = CORES * chips * rows * rows
    return pl.pallas_call(
        functools.partial(kernel, ctx_size, head_size),
        out_shape=(
            jax.ShapeDtypeStruct(query_in.shape, low),
            jax.ShapeDtypeStruct(key_in.shape, low),
            jax.ShapeDtypeStruct(value_in.shape, low),
        ),
        in_specs=[smem] + [hbm] * 5,
        out_specs=(vmem, vmem, vmem),
        scratch_shapes=[
            pltpu.VMEM(tokens, low),
            pltpu.VMEM(tokens, low),
            pltpu.VMEM((CORES, head_size, 1, block), jnp.float32),
            pltpu.VMEM(keys, low),
            pltpu.VMEM(keys, low),
            pltpu.VMEM((chips, rows, rows), jnp.float32),
            pltpu.VMEM(keys, low),
            pltpu.VMEM(keys, low),
            pltpu.VMEM(tokens, low),
            pltpu.VMEM(keys, low),
            pltpu.VMEM(keys, low),
            pltpu.VMEM((heads, token_rows, HEAD_DIM), low),
            pltpu.VMEM((token_rows, width), low),
            pltpu.VMEM((token_rows, width), low),
            pltpu.VMEM((heads, 1, block), jnp.float32),
            dma((copies,)),
            dma((2,)),
            dma((CORES, head_size)),
            dma((CORES, head_size)),
            dma((CORES, head_size)),
            dma((chips, CORES)),
            dma((chips, CORES)),
            dma((chips, CORES)),
            dma((chips, CORES)),
            dma((heads,)),
        ],
        compiler_params=pltpu.CompilerParams(
            collective_id=0, has_side_effects=True, vmem_limit_bytes=40 * 1024 * 1024
        ),
        cost_estimate=pl.CostEstimate(
            flops=5 * pairs * HEAD_DIM, bytes_accessed=10 * query_in.size, transcendentals=pairs
        ),
    )(span_place, query_in, key_in, value_in, out_saved, out_grad)


def solution(mesh):
    placed = (
        P(("ctx", "head"), None),
        P("ctx", "head"),
        P("ctx", "head"),
        P(("ctx", "head"), None),
        P(("ctx", "head"), None),
        P(),
    )
    return jax.shard_map(
        body,
        mesh=mesh,
        in_specs=placed,
        out_specs=(P(("ctx", "head"), None), P("ctx", "head"), P("ctx", "head")),
        check_vma=False,
    )
```

time: 99.8 us -> 29.3 us (0.29)
  waiting for transfers between devices: 36.3 us -> 0 us
  starting transfers between devices: 27.1 us -> 0 us
  Pallas kernels: 0 us -> 21.5 us
  blocking collectives: 19.9 us -> 0 us
  local copies, waits for them, and re-layouts: 11.8 us -> 6.73 us
  matrix products: 2.03 us -> 0 us
  other arithmetic: 1.04 us -> 0 us
    all_to_all x6 -> x0, waiting for transfers between devices: 36.3 us -> none  [the longest x1 13.9 us: body(): lax.all_to_all(stacked_k, 'ctx', split_axis=0, concat_axis=0, tiled=True)]
    all_to_all x6 -> x0, starting transfers between devices: 27.1 us -> none  [the longest x1 6.45 us: body(): lax.all_to_all(query_in, 'head', split_axis=1, concat_axis=0, tiled=True)]
    pallas_call x0 -> x1, Pallas kernels: none -> 21.5 us  [body(): pl.pallas_call(functools.partial(kernel, ctx_size, head_size), out_shape=...]
    all_gather x2 -> x0, blocking collectives: 19.9 us -> none  [the longest x1 9.99 us: body(): lax.all_gather(value_in, 'ctx', axis=0, tiled=True)]
    all_to_all x4 -> x0, local copies, waits for them, and re-layouts: 3.38 us -> none  [the longest x1 1.47 us: body(): lax.all_to_all(query_in, 'head', split_axis=1, concat_axis=0, tiled=True)]
    reshape x4 -> x0, local copies, waits for them, and re-layouts: 2.45 us -> none  [the longest x1 1.22 us: body(): stacked_v = partials[1].reshape(cycle_size, row_count, feature_width)]
    unnamed x16 -> x15, local copies, waits for them, and re-layouts: 4.42 us -> 6.73 us
    dot_general x5 -> x0, matrix products: 2.03 us -> none  [the longest x1 0.48 us: block_grads(): jnp.einsum('rhd,thd->hrt', grad_heads, value_heads, preferred_element_typ...]
  transfers between devices with their start and end apart: 6 -> 0, of which waited for: 4 -> 0; matrix products, arithmetic and copies ran while one was open for 8% -> 0% of each run, Pallas kernels for 0% -> 0%
where the time goes in v1:
time: 29.3 us; the launch traced here: 28.9 us
  Pallas kernels  21.5 us (73%)
  local copies, waits for them, and re-layouts  6.73 us (23%)
  between operations  0.65 us (2%)
    pallas_call x1, Pallas kernels, body(): pl.pallas_call(functools.partial(kernel, ctx_size, head_size), out_shape=...  21.5 us
    unnamed x15, local copies, waits for them, and re-layouts  6.73 us

profile of v1, /device:TPU:0, one launch (start us, length us, event | category | flops | bytes accessed | tf_op | source)
XLA Modules:
  0.0 28.9 jit_solution(2986302249587290674)
XLA Ops:
  0.6 0.0 copy-start
  0.6 0.8 %copy-done = bf16[32,1024]{1,0:T(8,128)(2,1)S(1)} copy-done((bf16[32,1024]{1,0:T(8,128)(2,1)S(1)}, bf16[32,1024]{1,0:T(8,128)(2,1)}, u32[]{:S(2)}) %copy-start) | copy-done | bytes 65560
  1.5 0.0 copy-start.1
  1.5 0.8 %copy-done.1 = bf16[128,256]{1,0:T(8,128)(2,1)S(1)} copy-done((bf16[128,256]{1,0:T(8,128)(2,1)S(1)}, bf16[128,256]{1,0:T(8,128)(2,1)}, u32[]{:S(2)}) %copy-start.1) | copy-done | bytes 65560
  2.3 0.0 copy-start.2
  2.3 0.8 %copy-done.2 = bf16[128,256]{1,0:T(8,128)(2,1)S(1)} copy-done((bf16[128,256]{1,0:T(8,128)(2,1)S(1)}, bf16[128,256]{1,0:T(8,128)(2,1)}, u32[]{:S(2)}) %copy-start.2) | copy-done | bytes 65560
  3.2 0.0 copy-start.3
  3.2 0.8 %copy-done.3 = bf16[32,1024]{1,0:T(8,128)(2,1)S(1)} copy-done((bf16[32,1024]{1,0:T(8,128)(2,1)S(1)}, bf16[32,1024]{1,0:T(8,128)(2,1)}, u32[]{:S(2)}) %copy-start.3) | copy-done | bytes 65560
  4.0 0.0 copy-start.4
  4.0 0.8 %copy-done.4 = bf16[32,1024]{1,0:T(8,128)(2,1)S(1)} copy-done((bf16[32,1024]{1,0:T(8,128)(2,1)S(1)}, bf16[32,1024]{1,0:T(8,128)(2,1)}, u32[]{:S(2)}) %copy-start.4) | copy-done | bytes 65560
  4.8 0.0 copy-start.5
  4.8 0.7 %copy-done.5 = s32[16]{0:T(128)S(1)} copy-done((s32[16]{0:T(128)S(1)}, s32[16]{0:T(128)}, u32[]{:S(2)}) %copy-start.5) | copy-done | bytes 88
  5.5 21.5 %shard_map.85 = (bf16[32,1024]{1,0:T(8,128)(2,1)S(1)}, bf16[128,256]{1,0:T(8,128)(2,1)S(1)}, bf16[128,256]{1,0:T(8,128)(2,1)S(1)}) custom-call(s32[16]{0:T(128)S(1)} %copy-done.5, bf16[32,1024]{1,0:T(8,128)(2,1)S(1)} %copy-done, bf16[128,256]{1,0:T(8,128)(2,1)S(1)} %copy-done.1, bf16[128,256]{1,0:T(8,128)(2,1)S(1)} %copy-done.2, ...), custom_call_target="tpu_custom_call" | custom-call | flops 335544320 | bytes 327680 | tf_op jit(solution)/shard_map/pallas_call | solution.py:235
  27.0 0.6 %copy.12 = bf16[32,1024]{1,0:T(8,128)(2,1)} copy(bf16[32,1024]{1,0:T(8,128)(2,1)S(1)} %get-tuple-element.6) | data formatting | bytes 131072
  27.7 0.6 %copy.13 = bf16[128,256]{1,0:T(8,128)(2,1)} copy(bf16[128,256]{1,0:T(8,128)(2,1)S(1)} %get-tuple-element.7) | data formatting | bytes 131072
  28.3 0.6 %copy.14 = bf16[128,256]{1,0:T(8,128)(2,1)} copy(bf16[128,256]{1,0:T(8,128)(2,1)S(1)} %get-tuple-element.8) | data formatting | bytes 131072
Async XLA Ops:
  0.6 0.8 %copy-start = (bf16[32,1024]{1,0:T(8,128)(2,1)S(1)}, bf16[32,1024]{1,0:T(8,128)(2,1)}, u32[]{:S(2)}) copy-start(bf16[32,1024]{1,0:T(8,128)(2,1)} %query_in.1) | copy-start | bytes 196612
  1.5 0.8 %copy-start.1 = (bf16[128,256]{1,0:T(8,128)(2,1)S(1)}, bf16[128,256]{1,0:T(8,128)(2,1)}, u32[]{:S(2)}) copy-start(bf16[128,256]{1,0:T(8,128)(2,1)} %key_in.1) | copy-start | bytes 196612
  2.3 0.8 %copy-start.2 = (bf16[128,256]{1,0:T(8,128)(2,1)S(1)}, bf16[128,256]{1,0:T(8,128)(2,1)}, u32[]{:S(2)}) copy-start(bf16[128,256]{1,0:T(8,128)(2,1)} %value_in.1) | copy-start | bytes 196612
  3.2 0.8 %copy-start.3 = (bf16[32,1024]{1,0:T(8,128)(2,1)S(1)}, bf16[32,1024]{1,0:T(8,128)(2,1)}, u32[]{:S(2)}) copy-start(bf16[32,1024]{1,0:T(8,128)(2,1)} %saved_in.1) | copy-start | bytes 196612
  4.0 0.8 %copy-start.4 = (bf16[32,1024]{1,0:T(8,128)(2,1)S(1)}, bf16[32,1024]{1,0:T(8,128)(2,1)}, u32[]{:S(2)}) copy-start(bf16[32,1024]{1,0:T(8,128)(2,1)} %grad_in.1) | copy-start | bytes 196612
  4.8 0.7 %copy-start.5 = (s32[16]{0:T(128)S(1)}, s32[16]{0:T(128)}, u32[]{:S(2)}) copy-start(s32[16]{0:T(128)} %place.1) | copy-start | bytes 196

commit v2 on v1

--- a/solution.py
+++ b/solution.py
@@ -10,6 +10,7 @@
 
 HEAD_DIM = 128
 CORES = 2
+GRANT = 56 * 1024 * 1024
 MESH = pl.DeviceIdType.MESH
 NT = (((1,), (1,)), ((), ()))
 NN = (((1,), (0,)), ((), ()))
@@ -25,10 +26,10 @@
 
 
 def kernel(
-    ctx_size, head_size, place, query_in, key_in, value_in, saved_in, grad_in,
+    ctx_size, head_size, place_in, query_in, key_in, value_in, saved_in, grad_in,
     dq_out, dk_out, dv_out,
-    qbuf, gbuf, dbuf, kbuf, vbuf, pbuf, dk_stage, dv_stage, dq_stage, kpart, vpart, qpart,
-    own_grad, own_saved, delta_src,
+    qbuf, gbuf, dbuf, kbuf, vbuf, pbuf, dk_stage, dv_stage, dq_stage, kpart, vpart, dk_total, dv_total,
+    own_grad, own_saved, delta_src, place,
     send_sem, local_sem, q_sem, g_sem, d_sem, k_sem, v_sem, kp_sem, vp_sem, qp_sem,
 ):
     chips = ctx_size // CORES
@@ -37,7 +38,7 @@
     token_rows = query_in.shape[0]
     heads = head_size * CORES
     rows = CORES * block
-    span = ctx_size * block // place.shape[0]
+    span = ctx_size * block // place_in.shape[0]
     spans = rows // span
     scale = HEAD_DIM ** -0.5
 
@@ -77,6 +78,8 @@
     saved_load = pltpu.make_async_copy(saved_in, own_saved, local_sem.at[1])
     grad_load.start()
     saved_load.start()
+    place_load = pltpu.make_async_copy(place_in, place, local_sem.at[2])
+    place_load.start()
     my_head = z * CORES + core
     pltpu.make_async_copy(query_in.at[:, columns(my_head)], qbuf.at[core, z], q_sem.at[core, z]).start()
     pltpu.make_async_copy(key_in.at[:, columns(core)], kbuf.at[chip, core], k_sem.at[chip, core]).start()
@@ -130,6 +133,8 @@
     for w, j in line:
         head = z_at[w] * CORES + core_at[j]
         send(delta_src.at[head], dbuf.at[core, z], d_sem.at[core, z], line_id(w, j))
+
+    place_load.wait()
 
     lane = lax.broadcasted_iota(jnp.int32, (1, rows), 1)
     place_row = jnp.zeros((1, rows), jnp.int32)
@@ -194,26 +199,39 @@
         grad_q += matmul(dscores, kbuf[chip_at[c]].reshape(rows, HEAD_DIM), TN)
 
     dq_stage[...] = grad_q.astype(jnp.bfloat16).reshape(dq_stage.shape)
-    qpart[my_head] = dq_stage[core, z]
     for w, j in line:
-        send(dq_stage.at[core_at[j], z_at[w]], qpart.at[my_head], qp_sem.at[my_head], line_id(w, j))
-
-    for part, sem, out in ((vpart, vp_sem, dv_out), (kpart, kp_sem, dk_out)):
+        dst = dq_out.at[:, columns(my_head)]
+        send(dq_stage.at[core_at[j], z_at[w]], dst, qp_sem.at[my_head], line_id(w, j))
+    own = pltpu.make_async_copy(dq_stage.at[core, z], dq_out.at[:, columns(my_head)], qp_sem.at[my_head])
+    own.start()
+
+    stores = []
+    for part, sem, total, out in ((vpart, vp_sem, dv_total, dv_out), (kpart, kp_sem, dk_total, dk_out)):
         for c, j in plane:
             arrive(part.at[chip_at[c], core_at[j]], sem.at[chip_at[c], core_at[j]])
         for j in range(CORES):
             summed = part[0, j].astype(jnp.float32)
             for c in range(1, chips):
                 summed += part[c, j].astype(jnp.float32)
-            out[:, j * HEAD_DIM : (j + 1) * HEAD_DIM] = summed.astype(jnp.bfloat16)
-
-    for w, j in line:
-        head = z_at[w] * CORES + core_at[j]
-        arrive(qpart.at[head], qp_sem.at[head])
+            total[:, j * HEAD_DIM : (j + 1) * HEAD_DIM] = summed.astype(jnp.bfloat16)
+        stores.append(pltpu.make_async_copy(total, out, local_sem.at[len(stores)]))
+        stores[-1].start()
+
     for h in range(heads):
-        dq_out[:, h * HEAD_DIM : (h + 1) * HEAD_DIM] = qpart[h]
+        arrive(dq_out.at[:, h * HEAD_DIM : (h + 1) * HEAD_DIM], qp_sem.at[h])
+    for copy in stores:
+        copy.wait()
     for copy in sent:
         copy.wait_send()
+
+
+def store_kernel(dq, dk, dv, dq_out, dk_out, dv_out, sem):
+    pairs = ((dq, dq_out), (dk, dk_out), (dv, dv_out))
+    copies = [pltpu.make_async_copy(src, dst, sem.at[i]) for i, (src, dst) in enumerate(pairs)]
+    for copy in copies:
+        copy.start()
+    for copy in copies:
+        copy.wait()
 
 
 def body(query_in, key_in, value_in, out_saved, out_grad, span_place):
@@ -228,19 +246,17 @@
     keys = (chips, CORES, block, HEAD_DIM)
     dma = pltpu.SemaphoreType.DMA
     copies = 4 * (ctx_size - 1) + 4 * (heads - 1)
-    vmem = pl.BlockSpec(memory_space=pltpu.VMEM)
-    hbm = pl.BlockSpec(memory_space=pl.ANY)
-    smem = pl.BlockSpec(memory_space=pltpu.SMEM)
+    hbm = pl.BlockSpec(memory_space=pltpu.HBM)
     pairs = CORES * chips * rows * rows
-    return pl.pallas_call(
+    grads = pl.pallas_call(
         functools.partial(kernel, ctx_size, head_size),
         out_shape=(
             jax.ShapeDtypeStruct(query_in.shape, low),
             jax.ShapeDtypeStruct(key_in.shape, low),
             jax.ShapeDtypeStruct(value_in.shape, low),
         ),
-        in_specs=[smem] + [hbm] * 5,
-        out_specs=(vmem, vmem, vmem),
+        in_specs=[hbm] * 6,
+        out_specs=(hbm, hbm, hbm),
         scratch_shapes=[
             pltpu.VMEM(tokens, low),
             pltpu.VMEM(tokens, low),
@@ -253,12 +269,14 @@
             pltpu.VMEM(tokens, low),
             pltpu.VMEM(keys, low),
             pltpu.VMEM(keys, low),
-            pltpu.VMEM((heads, token_rows, HEAD_DIM), low),
+            pltpu.VMEM(key_in.shape, low),
+            pltpu.VMEM(value_in.shape, low),
             pltpu.VMEM((token_rows, width), low),
             pltpu.VMEM((token_rows, width), low),
             pltpu.VMEM((heads, 1, block), jnp.float32),
+            pltpu.SMEM(span_place.shape, span_place.dtype),
             dma((copies,)),
-            dma((2,)),
+            dma((3,)),
             dma((CORES, head_size)),
             dma((CORES, head_size)),
             dma((CORES, head_size)),
@@ -269,12 +287,20 @@
             dma((heads,)),
         ],
         compiler_params=pltpu.CompilerParams(
-            collective_id=0, has_side_effects=True, vmem_limit_bytes=40 * 1024 * 1024
+            collective_id=0, has_side_effects=True, vmem_limit_bytes=GRANT
         ),
         cost_estimate=pl.CostEstimate(
             flops=5 * pairs * HEAD_DIM, bytes_accessed=10 * query_in.size, transcendentals=pairs
         ),
     )(span_place, query_in, key_in, value_in, out_saved, out_grad)
+    return pl.pallas_call(
+        store_kernel,
+        out_shape=tuple(jax.ShapeDtypeStruct(g.shape, g.dtype) for g in grads),
+        in_specs=[hbm] * 3,
+        out_specs=(hbm, hbm, hbm),
+        scratch_shapes=[dma((3,))],
+        compiler_params=pltpu.CompilerParams(vmem_limit_bytes=GRANT),
+    )(*grads)
 
 
 def solution(mesh):

time: 29.3 us -> 29.7 us (1.014)
  Pallas kernels: 21.5 us -> 28.9 us
  local copies, waits for them, and re-layouts: 6.73 us -> 0 us
    pallas_call x0 -> x1, Pallas kernels: none -> 7.09 us  [body(): pl.pallas_call(store_kernel, out_shape=tuple((jax.ShapeDtypeStruct(g.shap...]
    unnamed x15 -> x0, local copies, waits for them, and re-layouts: 6.73 us -> none
where the time goes in v2:
time: 29.7 us; the launch traced here: 29.6 us
  Pallas kernels  28.9 us (97%)
  between operations  0.64 us (2%)
    pallas_call x1, Pallas kernels, body(): pl.pallas_call(functools.partial(kernel, ctx_size, head_size), out_shape=...  21.8 us
    pallas_call x1, Pallas kernels, body(): pl.pallas_call(store_kernel, out_shape=tuple((jax.ShapeDtypeStruct(g.shap...  7.09 us

profile of v2, /device:TPU:0, one launch (start us, length us, event | category | flops | bytes accessed | tf_op | source)
XLA Modules:
  0.0 29.6 jit_solution(8720766268762862503)
XLA Ops:
  0.6 21.8 %shard_map.85 = (bf16[32,1024]{1,0:T(8,128)(2,1)}, bf16[128,256]{1,0:T(8,128)(2,1)}, bf16[128,256]{1,0:T(8,128)(2,1)}) custom-call(s32[16]{0:T(128)} %place_in.1, bf16[32,1024]{1,0:T(8,128)(2,1)} %query_in.1, bf16[128,256]{1,0:T(8,128)(2,1)} %key_in.1, bf16[128,256]{1,0:T(8,128)(2,1)} %value_in.1, bf16[32,1024]{1,0:T(8,128)(2,1)} %saved_in.1, ...), custom_call_target="tpu_custom_call" | custom-call | flops 335544320 | bytes 327680 | tf_op jit(solution)/shard_map/pallas_call | solution.py:251
  22.5 7.1 %shard_map.86 = (bf16[32,1024]{1,0:T(8,128)(2,1)}, bf16[128,256]{1,0:T(8,128)(2,1)}, bf16[128,256]{1,0:T(8,128)(2,1)}) custom-call(bf16[32,1024]{1,0:T(8,128)(2,1)} %get-tuple-element.6.dq, bf16[128,256]{1,0:T(8,128)(2,1)} %get-tuple-element.7.dk, bf16[128,256]{1,0:T(8,128)(2,1)} %get-tuple-element.8.dv), custom_call_target="tpu_custom_call" | custom-call | tf_op jit(solution)/shard_map/pallas_call | solution.py:296

commit v3 on v2

--- a/solution.py
+++ b/solution.py
@@ -27,8 +27,8 @@
 
 def kernel(
     ctx_size, head_size, place_in, query_in, key_in, value_in, saved_in, grad_in,
-    dq_out, dk_out, dv_out,
-    qbuf, gbuf, dbuf, kbuf, vbuf, pbuf, dk_stage, dv_stage, dq_stage, kpart, vpart, dk_total, dv_total,
+    dq_out, kpart, vpart,
+    qbuf, gbuf, dbuf, kbuf, vbuf, pbuf, dk_stage, dv_stage, dq_stage,
     own_grad, own_saved, delta_src, place,
     send_sem, local_sem, q_sem, g_sem, d_sem, k_sem, v_sem, kp_sem, vp_sem, qp_sem,
 ):
@@ -195,7 +195,7 @@
                 if c or j:
                     send(stage.at[c, core_at[j]], part.at[chip, core], sem.at[chip, core], plane_id(c, j))
                 else:
-                    part[chip, core] = stage[c, core]
+                    pltpu.make_async_copy(stage.at[c, core], part.at[chip, core], sem.at[chip, core]).start()
         grad_q += matmul(dscores, kbuf[chip_at[c]].reshape(rows, HEAD_DIM), TN)
 
     dq_stage[...] = grad_q.astype(jnp.bfloat16).reshape(dq_stage.shape)
@@ -205,33 +205,38 @@
     own = pltpu.make_async_copy(dq_stage.at[core, z], dq_out.at[:, columns(my_head)], qp_sem.at[my_head])
     own.start()
 
-    stores = []
-    for part, sem, total, out in ((vpart, vp_sem, dv_total, dv_out), (kpart, kp_sem, dk_total, dk_out)):
-        for c, j in plane:
-            arrive(part.at[chip_at[c], core_at[j]], sem.at[chip_at[c], core_at[j]])
-        for j in range(CORES):
-            summed = part[0, j].astype(jnp.float32)
-            for c in range(1, chips):
-                summed += part[c, j].astype(jnp.float32)
-            total[:, j * HEAD_DIM : (j + 1) * HEAD_DIM] = summed.astype(jnp.bfloat16)
-        stores.append(pltpu.make_async_copy(total, out, local_sem.at[len(stores)]))
-        stores[-1].start()
-
+    for part, sem in ((vpart, vp_sem), (kpart, kp_sem)):
+        for c in range(chips):
+            for j in range(CORES):
+                arrive(part.at[c, j], sem.at[c, j])
     for h in range(heads):
         arrive(dq_out.at[:, h * HEAD_DIM : (h + 1) * HEAD_DIM], qp_sem.at[h])
-    for copy in stores:
-        copy.wait()
     for copy in sent:
         copy.wait_send()
 
 
-def store_kernel(dq, dk, dv, dq_out, dk_out, dv_out, sem):
-    pairs = ((dq, dq_out), (dk, dk_out), (dv, dv_out))
-    copies = [pltpu.make_async_copy(src, dst, sem.at[i]) for i, (src, dst) in enumerate(pairs)]
-    for copy in copies:
-        copy.start()
-    for copy in copies:
-        copy.wait()
+def sum_kernel(dq, kpart, vpart, dq_out, dk_out, dv_out, dq_buf, kbuf, vbuf, dk_buf, dv_buf, load_sem, store_sem):
+    loads = [
+        pltpu.make_async_copy(src, dst, load_sem.at[i])
+        for i, (src, dst) in enumerate(((vpart, vbuf), (kpart, kbuf), (dq, dq_buf)))
+    ]
+    for load in loads:
+        load.start()
+    stores = []
+    for load, parts, total, out in ((loads[0], vbuf, dv_buf, dv_out), (loads[1], kbuf, dk_buf, dk_out)):
+        load.wait()
+        for j in range(parts.shape[1]):
+            summed = parts[0, j].astype(jnp.float32)
+            for c in range(1, parts.shape[0]):
+                summed += parts[c, j].astype(jnp.float32)
+            total[:, j * HEAD_DIM : (j + 1) * HEAD_DIM] = summed.astype(jnp.bfloat16)
+        stores.append(pltpu.make_async_copy(total, out, store_sem.at[len(stores)]))
+        stores[-1].start()
+    loads[2].wait()
+    stores.append(pltpu.make_async_copy(dq_buf, dq_out, store_sem.at[2]))
+    stores[-1].start()
+    for store in stores:
+        store.wait()
 
 
 def body(query_in, key_in, value_in, out_saved, out_grad, span_place):
@@ -252,8 +257,8 @@
         functools.partial(kernel, ctx_size, head_size),
         out_shape=(
             jax.ShapeDtypeStruct(query_in.shape, low),
-            jax.ShapeDtypeStruct(key_in.shape, low),
-            jax.ShapeDtypeStruct(value_in.shape, low),
+            jax.ShapeDtypeStruct(keys, low),
+            jax.ShapeDtypeStruct(keys, low),
         ),
         in_specs=[hbm] * 6,
         out_specs=(hbm, hbm, hbm),
@@ -267,10 +272,6 @@
             pltpu.VMEM(keys, low),
             pltpu.VMEM(keys, low),
             pltpu.VMEM(tokens, low),
-            pltpu.VMEM(keys, low),
-            pltpu.VMEM(keys, low),
-            pltpu.VMEM(key_in.shape, low),
-            pltpu.VMEM(value_in.shape, low),
             pltpu.VMEM((token_rows, width), low),
             pltpu.VMEM((token_rows, width), low),
             pltpu.VMEM((heads, 1, block), jnp.float32),
@@ -293,12 +294,21 @@
             flops=5 * pairs * HEAD_DIM, bytes_accessed=10 * query_in.size, transcendentals=pairs
         ),
     )(span_place, query_in, key_in, value_in, out_saved, out_grad)
+    shapes = (query_in.shape, key_in.shape, value_in.shape)
     return pl.pallas_call(
-        store_kernel,
-        out_shape=tuple(jax.ShapeDtypeStruct(g.shape, g.dtype) for g in grads),
+        sum_kernel,
+        out_shape=tuple(jax.ShapeDtypeStruct(shape, low) for shape in shapes),
         in_specs=[hbm] * 3,
         out_specs=(hbm, hbm, hbm),
-        scratch_shapes=[dma((3,))],
+        scratch_shapes=[
+            pltpu.VMEM(query_in.shape, low),
+            pltpu.VMEM(keys, low),
+            pltpu.VMEM(keys, low),
+            pltpu.VMEM(key_in.shape, low),
+            pltpu.VMEM(value_in.shape, low),
+            dma((3,)),
+            dma((3,)),
+        ],
         compiler_params=pltpu.CompilerParams(vmem_limit_bytes=GRANT),
     )(*grads)
 

time: 29.7 us -> 23.9 us (0.80)
  Pallas kernels: 28.9 us -> 23.1 us
    pallas_call x1, Pallas kernels: 7.09 us -> 1.77 us  [body(): pl.pallas_call(sum_kernel, out_shape=tuple((jax.ShapeDtypeStruct(shape, l...]
    pallas_call x1, Pallas kernels: 21.8 us -> 21.3 us  [body(): pl.pallas_call(functools.partial(kernel, ctx_size, head_size), out_shape=...]
where the time goes in v3:
time: 23.9 us; the launch traced here: 23.7 us
  Pallas kernels  23.1 us (97%)
  between operations  0.64 us (3%)
    pallas_call x1, Pallas kernels, body(): pl.pallas_call(functools.partial(kernel, ctx_size, head_size), out_shape=...  21.3 us
    pallas_call x1, Pallas kernels, body(): pl.pallas_call(sum_kernel, out_shape=tuple((jax.ShapeDtypeStruct(shape, l...  1.77 us

profile of v3, /device:TPU:0, one launch (start us, length us, event | category | flops | bytes accessed | tf_op | source)
XLA Modules:
  0.0 23.7 jit_solution(18218444913797048196)
XLA Ops:
  0.6 21.3 %shard_map.85 = (bf16[32,1024]{1,0:T(8,128)(2,1)}, bf16[4,2,128,128]{3,2,1,0:T(8,128)(2,1)}, bf16[4,2,128,128]{3,2,1,0:T(8,128)(2,1)}) custom-call(s32[16]{0:T(128)} %place_in.1, bf16[32,1024]{1,0:T(8,128)(2,1)} %query_in.1, bf16[128,256]{1,0:T(8,128)(2,1)} %key_in.1, bf16[128,256]{1,0:T(8,128)(2,1)} %value_in.1, bf16[32,1024]{1,0:T(8,128)(2,1)} %saved_in.1, ...), custom_call_target="tpu_custom_call" | custom-call | flops 335544320 | bytes 327680 | tf_op jit(solution)/shard_map/pallas_call | solution.py:256
  21.9 1.8 %shard_map.86 = (bf16[32,1024]{1,0:T(8,128)(2,1)}, bf16[128,256]{1,0:T(8,128)(2,1)}, bf16[128,256]{1,0:T(8,128)(2,1)}) custom-call(bf16[32,1024]{1,0:T(8,128)(2,1)} %get-tuple-element.6.dq, bf16[4,2,128,128]{3,2,1,0:T(8,128)(2,1)} %get-tuple-element.7.kpart, bf16[4,2,128,128]{3,2,1,0:T(8,128)(2,1)} %get-tuple-element.8.vpart), custom_call_target="tpu_custom_call" | custom-call | tf_op jit(solution)/shard_map/pallas_call | solution.py:298

commit v4 on v3

v4 whole, which is shorter than its diff:
```python
import functools
import math

import jax
import jax.numpy as jnp
from jax import lax
from jax.experimental import pallas as pl
from jax.experimental.pallas import tpu as pltpu
from jax.sharding import PartitionSpec as P

HEAD_DIM = 128
CORES = 2
SIDES = 2
GRANT = 56 * 1024 * 1024
MESH = pl.DeviceIdType.MESH
NT = (((1,), (1,)), ((), ()))
NN = (((1,), (0,)), ((), ()))
TN = (((0,), (0,)), ((), ()))


def matmul(a, b, dims):
    return lax.dot_general(a, b, dims, preferred_element_type=jnp.float32)


def columns(index):
    return pl.ds(pl.multiple_of(index * HEAD_DIM, HEAD_DIM), HEAD_DIM)


def kernel(
    ctx_size, head_size, place_in, query_in, key_in, value_in, saved_in, grad_in,
    qpart, kpart, vpart,
    qbuf, gbuf, dbuf, kbuf, vbuf, pbuf, dpbuf, plow, dslow, dk_stage, dv_stage, dq_stage,
    own_grad, own_saved, delta_src, stat_src, stat_got, place,
    send_sem, local_sem, q_sem, g_sem, d_sem, k_sem, v_sem, relay_sem, stat_sem, kp_sem, vp_sem, qp_sem,
):
    groups = kbuf.shape[0]
    block = key_in.shape[0]
    token_rows = query_in.shape[0]
    heads = head_size * CORES
    rows = CORES * block
    span = ctx_size * block // place_in.shape[0]
    spans = rows // span
    scale = HEAD_DIM ** -0.5

    me = lax.axis_index("ctx")
    z = lax.axis_index("head")
    core = lax.rem(me, CORES)
    chip = me // CORES
    low, high = lax.rem(chip, SIDES), chip // SIDES

    group_at = [lax.rem(high + step, groups) for step in range(groups)]
    side_at = [lax.rem(low + step, SIDES) for step in range(SIDES)]
    core_at = [lax.rem(core + step, CORES) for step in range(CORES)]
    z_at = [lax.rem(z + step, head_size) for step in range(head_size)]
    column = [(g, j) for g in range(groups) for j in range(CORES) if g or j]
    line = [(w, j) for w in range(head_size) for j in range(CORES) if w or j]
    every = [(w, j) for w in range(head_size) for j in range(CORES)]

    def column_id(g, j):
        return {"ctx": (group_at[g] * SIDES + low) * CORES + core_at[j], "head": z}

    def line_id(w, j, side=0):
        return {"ctx": (high * SIDES + side_at[side]) * CORES + core_at[j], "head": z_at[w]}

    barrier = pltpu.get_barrier_semaphore()
    peers = [column_id(g, j) for g, j in column] + [line_id(w, j) for w, j in line if w]
    peers += [line_id(w, j, 1) for w, j in every]
    for peer in peers:
        pl.semaphore_signal(barrier, inc=1, device_id=peer, device_id_type=MESH)

    grad_load = pltpu.make_async_copy(grad_in, own_grad, local_sem.at[0])
    saved_load = pltpu.make_async_copy(saved_in, own_saved, local_sem.at[1])
    grad_load.start()
    saved_load.start()
    place_load = pltpu.make_async_copy(place_in, place, local_sem.at[2])
    place_load.start()
    my_head = z * CORES + core
    pltpu.make_async_copy(query_in.at[:, columns(my_head)], qbuf.at[low, core, z], q_sem.at[core, z]).start()
    pltpu.make_async_copy(key_in.at[:, columns(core)], kbuf.at[high, core], k_sem.at[high, core]).start()
    pltpu.make_async_copy(grad_in.at[:, columns(my_head)], gbuf.at[low, core, z], g_sem.at[core, z]).start()
    pltpu.make_async_copy(value_in.at[:, columns(core)], vbuf.at[high, core], v_sem.at[high, core]).start()

    grad_load.wait()
    saved_load.wait()
    product = own_grad[...].astype(jnp.float32) * own_saved[...].astype(jnp.float32)
    coarse = product.astype(jnp.bfloat16)
    fine = (product - coarse.astype(jnp.float32)).astype(jnp.bfloat16)
    shape = (heads, heads * HEAD_DIM)
    member = lax.broadcasted_iota(jnp.int32, shape, 1) // HEAD_DIM == lax.broadcasted_iota(jnp.int32, shape, 0)
    member = jnp.where(member, 1.0, 0.0).astype(jnp.bfloat16)
    delta = matmul(member, jnp.concatenate([coarse] * head_size, axis=0), NT)
    delta += matmul(member, jnp.concatenate([fine] * head_size, axis=0), NT)
    lane_z = lax.broadcasted_iota(jnp.int32, (heads, block), 1) // token_rows
    delta = jnp.where(lane_z == z, delta, 0.0)
    for h in range(heads):
        delta_src[h] = delta[h : h + 1]
    dbuf[core, z] = delta_src[my_head]

    pl.semaphore_wait(barrier, len(peers))

    sent = []

    def send(src, dst, sem, device):
        copy = pltpu.make_async_remote_copy(
            src_ref=src, dst_ref=dst, send_sem=send_sem.at[len(sent)], recv_sem=sem,
            device_id=device, device_id_type=MESH,
        )
        copy.start()
        sent.append(copy)

    def arrive(dst, sem):
        pltpu.make_async_copy(dst, dst, sem).wait()

    def send_column(src, dst, sem):
        for g, j in column[::-1]:
            send(src.at[:, columns(core_at[j])], dst.at[high, core], sem.at[high, core], column_id(g, j))

    def send_line(src, dst, sem):
        for w, j in line:
            head = z_at[w] * CORES + core_at[j]
            send(src.at[:, columns(head)], dst.at[low, core, z], sem.at[core, z], line_id(w, j))

    def relay(buf, sem, first):
        for j in range(CORES):
            for w in range(head_size):
                arrive(buf.at[low, j, w], sem.at[j, w])
            send(buf.at[low, j], buf.at[low, j], relay_sem.at[first + j], line_id(0, 0, 1))

    def relayed(buf, first):
        for j in range(CORES):
            arrive(buf.at[side_at[1], j], relay_sem.at[first + j])

    def rows_of(buf, index):
        return buf[index].reshape(rows, HEAD_DIM)

    send_line(query_in, qbuf, q_sem)
    send_column(key_in, kbuf, k_sem)
    for w, j in line:
        head = z_at[w] * CORES + core_at[j]
        send(delta_src.at[head], dbuf.at[core, z], d_sem.at[core, z], line_id(w, j))
    send_line(grad_in, gbuf, g_sem)
    send_column(value_in, vbuf, v_sem)
    place_load.wait()

    lane = lax.broadcasted_iota(jnp.int32, (1, rows), 1)
    pos_row = []
    for side in range(SIDES):
        place_row = jnp.zeros((1, rows), jnp.int32)
        for s in range(spans):
            here = place[(high * SIDES + side_at[side]) * spans + s]
            place_row = jnp.where(lane // span == s, here, place_row)
        pos_row.append(place_row * span + lane % span)
    within = lax.broadcasted_iota(jnp.int32, (span, rows), 0)

    stats, tops = [], []
    for side in range(SIDES):
        if side == 0:
            relay(qbuf, q_sem, 0)
        else:
            relayed(qbuf, 0)
        query = rows_of(qbuf, side_at[side])
        side_tops, sums = [], []
        for g in range(groups):
            if side == 0:
                for j in range(CORES):
                    arrive(kbuf.at[group_at[g], j], k_sem.at[group_at[g], j])
            scores = matmul(rows_of(kbuf, group_at[g]), query, NT) * (scale * math.log2(math.e))
            pieces = []
            for s in range(spans):
                limit = pos_row[side] - place[(group_at[g] * SIDES + low) * spans + s] * span
                pieces.append(jnp.where(within <= limit, scores[s * span : (s + 1) * span], -1e30))
            masked = jnp.concatenate(pieces, axis=0)
            top = jnp.max(masked, axis=0, keepdims=True)
            probs = jnp.exp2(masked - top)
            pbuf[g, side] = probs
            side_tops.append(top)
            sums.append(jnp.sum(probs, axis=0, keepdims=True))
        best = functools.reduce(jnp.maximum, side_tops)
        total = functools.reduce(jnp.add, [jnp.exp2(t - best) * s for t, s in zip(side_tops, sums)])
        stats.append((best, total))
        tops.append(side_tops)

    for w, j in line:
        arrive(dbuf.at[core_at[j], z_at[w]], d_sem.at[core_at[j], z_at[w]])
    own_delta = jnp.concatenate(
        [functools.reduce(jnp.add, [dbuf[j, w] for w in range(head_size)]) for j in range(CORES)], axis=1
    )
    stat_src[...] = jnp.concatenate([*stats[0], *stats[1], own_delta, own_delta, own_delta, own_delta], axis=0)
    send(stat_src, stat_got, stat_sem.at[0], line_id(0, 0, 1))
    relay(gbuf, g_sem, CORES)

    for side in range(SIDES):
        if side:
            relayed(gbuf, CORES)
        grad = rows_of(gbuf, side_at[side])
        for g in range(groups):
            if side == 0:
                for j in range(CORES):
                    arrive(vbuf.at[group_at[g], j], v_sem.at[group_at[g], j])
            dpbuf[g, side] = matmul(rows_of(vbuf, group_at[g]), grad, NT)

    arrive(stat_got, stat_sem.at[0])
    got = stat_got[...]
    deltas = (own_delta, got[4:5])
    weights = []
    for side in range(SIDES):
        best, total = stats[side]
        their = 2 * (SIDES - 1 - side)
        their_best, their_total = got[their : their + 1], got[their + 1 : their + 2]
        top = jnp.maximum(best, their_best)
        total = total * jnp.exp2(best - top) + their_total * jnp.exp2(their_best - top)
        weights.append([jnp.exp2(t - top) / total for t in tops[side]])

    for side in range(SIDES)[::-1]:
        grad_q = jnp.zeros((rows, HEAD_DIM), jnp.float32)
        for g in range(groups):
            probs = pbuf[g, side] * weights[side][g]
            plow[g, side] = probs.astype(jnp.bfloat16)
            dscores = (probs * (dpbuf[g, side] - deltas[side]) * scale).astype(jnp.bfloat16)
            dslow[g, side] = dscores
            grad_q += matmul(dscores, rows_of(kbuf, group_at[g]), TN)
        dq_stage[side] = grad_q.astype(jnp.bfloat16).reshape(dq_stage.shape[1:])
        for w, j in every[::-1]:
            src, dst, sem = dq_stage.at[side, core_at[j], z_at[w]], qpart.at[low, my_head], qp_sem.at[low, my_head]
            if side or w or j:
                send(src, dst, sem, line_id(w, j, side))
            else:
                pltpu.make_async_copy(src, dst, sem).start()

    for g in range(groups)[::-1]:
        for low_part, stage, buf, part, sem in (
            (plow, dv_stage, gbuf, vpart, vp_sem),
            (dslow, dk_stage, qbuf, kpart, kp_sem),
        ):
            total = matmul(low_part[g, 0], rows_of(buf, side_at[0]), NN)
            total += matmul(low_part[g, 1], rows_of(buf, side_at[1]), NN)
            stage[g] = total.astype(jnp.bfloat16).reshape(stage.shape[1:])
            for j in range(CORES):
                src, dst = stage.at[g, core_at[j]], part.at[high, core]
                if g or j:
                    send(src, dst, sem.at[high, core], column_id(g, j))
                else:
                    pltpu.make_async_copy(src, dst, sem.at[high, core]).start()

    for part, sem in ((vpart, vp_sem), (kpart, kp_sem)):
        for g in range(groups):
            for j in range(CORES):
                arrive(part.at[g, j], sem.at[g, j])
    for side in range(SIDES):
        for h in range(heads):
            arrive(qpart.at[side, h], qp_sem.at[side, h])
    for copy in sent:
        copy.wait_send()


def sum_kernel(
    qpart, kpart, vpart, dq_out, dk_out, dv_out, qbuf, kbuf, vbuf, dq_buf, dk_buf, dv_buf, load_sem, store_sem
):
    loads = [
        pltpu.make_async_copy(src, dst, load_sem.at[i])
        for i, (src, dst) in enumerate(((vpart, vbuf), (kpart, kbuf), (qpart, qbuf)))
    ]
    for load in loads:
        load.start()
    stores = []
    for load, parts, total, out in ((loads[0], vbuf, dv_buf, dv_out), (loads[1], kbuf, dk_buf, dk_out)):
        load.wait()
        for j in range(parts.shape[1]):
            summed = parts[0, j].astype(jnp.float32)
            for c in range(1, parts.shape[0]):
                summed += parts[c, j].astype(jnp.float32)
            total[:, j * HEAD_DIM : (j + 1) * HEAD_DIM] = summed.astype(jnp.bfloat16)
        stores.append(pltpu.make_async_copy(total, out, store_sem.at[len(stores)]))
        stores[-1].start()
    loads[2].wait()
    for h in range(qbuf.shape[1]):
        summed = functools.reduce(jnp.add, [qbuf[side, h].astype(jnp.float32) for side in range(SIDES)])
        dq_buf[:, h * HEAD_DIM : (h + 1) * HEAD_DIM] = summed.astype(jnp.bfloat16)
    stores.append(pltpu.make_async_copy(dq_buf, dq_out, store_sem.at[2]))
    stores[-1].start()
    for store in stores:
        store.wait()


def body(query_in, key_in, value_in, out_saved, out_grad, span_place):
    ctx_size, head_size = lax.axis_size("ctx"), lax.axis_size("head")
    groups = ctx_size // (CORES * SIDES)
    block = key_in.shape[0]
    token_rows, width = query_in.shape
    heads = head_size * CORES
    rows = CORES * block
    low = jnp.bfloat16
    tokens = (SIDES, CORES, head_size, token_rows, HEAD_DIM)
    keys = (groups, CORES, block, HEAD_DIM)
    pieces = (SIDES, heads, token_rows, HEAD_DIM)
    tiles = (groups, SIDES, rows, rows)
    dma = pltpu.SemaphoreType.DMA
    copies = 4 * (CORES * groups - 1) + 3 * (heads - 1) + 2 * CORES + 1 + SIDES * heads - 1
    hbm = pl.BlockSpec(memory_space=pltpu.HBM)
    pairs = groups * SIDES * rows * rows
    grads = pl.pallas_call(
        functools.partial(kernel, ctx_size, head_size),
        out_shape=(
            jax.ShapeDtypeStruct(pieces, low),
            jax.ShapeDtypeStruct(keys, low),
            jax.ShapeDtypeStruct(keys, low),
        ),
        in_specs=[hbm] * 6,
        out_specs=(hbm, hbm, hbm),
        scratch_shapes=[
            pltpu.VMEM(tokens, low),
            pltpu.VMEM(tokens, low),
            pltpu.VMEM((CORES, head_size, 1, block), jnp.float32),
            pltpu.VMEM(keys, low),
            pltpu.VMEM(keys, low),
            pltpu.VMEM(tiles, jnp.float32),
            pltpu.VMEM(tiles, jnp.float32),
            pltpu.VMEM(tiles, low),
            pltpu.VMEM(tiles, low),
            pltpu.VMEM(keys, low),
            pltpu.VMEM(keys, low),
            pltpu.VMEM(tokens, low),
            pltpu.VMEM((token_rows, width), low),
            pltpu.VMEM((token_rows, width), low),
            pltpu.VMEM((heads, 1, block), jnp.float32),
            pltpu.VMEM((8, rows), jnp.float32),
            pltpu.VMEM((8, rows), jnp.float32),
            pltpu.SMEM(span_place.shape, span_place.dtype),
            dma((copies,)),
            dma((3,)),
            dma((CORES, head_size)),
            dma((CORES, head_size)),
            dma((CORES, head_size)),
            dma((groups, CORES)),
            dma((groups, CORES)),
            dma((2 * CORES,)),
            dma((1,)),
            dma((groups, CORES)),
            dma((groups, CORES)),
            dma((SIDES, heads)),
        ],
        compiler_params=pltpu.CompilerParams(
            collective_id=0, has_side_effects=True, vmem_limit_bytes=GRANT
        ),
        cost_estimate=pl.CostEstimate(
            flops=5 * pairs * HEAD_DIM, bytes_accessed=10 * query_in.size, transcendentals=pairs
        ),
    )(span_place, query_in, key_in, value_in, out_saved, out_grad)
    shapes = (query_in.shape, key_in.shape, value_in.shape)
    return pl.pallas_call(
        sum_kernel,
        out_shape=tuple(jax.ShapeDtypeStruct(shape, low) for shape in shapes),
        in_specs=[hbm] * 3,
        out_specs=(hbm, hbm, hbm),
        scratch_shapes=[
            pltpu.VMEM(pieces, low),
            pltpu.VMEM(keys, low),
            pltpu.VMEM(keys, low),
            pltpu.VMEM(query_in.shape, low),
            pltpu.VMEM(key_in.shape, low),
            pltpu.VMEM(value_in.shape, low),
            dma((3,)),
            dma((3,)),
        ],
        compiler_params=pltpu.CompilerParams(vmem_limit_bytes=GRANT),
    )(*grads)


def solution(mesh):
    placed = (
        P(("ctx", "head"), None),
        P("ctx", "head"),
        P("ctx", "head"),
        P(("ctx", "head"), None),
        P(("ctx", "head"), None),
        P(),
    )
    return jax.shard_map(
        body,
        mesh=mesh,
        in_specs=placed,
        out_specs=(P(("ctx", "head"), None), P("ctx", "head"), P("ctx", "head")),
        check_vma=False,
    )
```

time: 23.9 us -> 26.6 us (1.11)
  Pallas kernels: 23.1 us -> 25.7 us
    pallas_call x1, Pallas kernels: 21.3 us -> 24 us  [body(): pl.pallas_call(functools.partial(kernel, ctx_size, head_size), out_shape=...]
where the time goes in v4:
time: 26.6 us; the launch traced here: 26.4 us
  Pallas kernels  25.7 us (97%)
  between operations  0.64 us (2%)
    pallas_call x1, Pallas kernels, body(): pl.pallas_call(functools.partial(kernel, ctx_size, head_size), out_shape=...  24 us
    pallas_call x1, Pallas kernels, body(): pl.pallas_call(sum_kernel, out_shape=tuple((jax.ShapeDtypeStruct(shape, l...  1.73 us

profile of v4, /device:TPU:0, one launch (start us, length us, event | category | flops | bytes accessed | tf_op | source)
XLA Modules:
  0.0 26.4 jit_solution(4589952001106501990)
XLA Ops:
  0.6 24.0 %shard_map.85 = (bf16[2,8,32,128]{3,2,1,0:T(8,128)(2,1)}, bf16[2,2,128,128]{3,2,1,0:T(8,128)(2,1)}, bf16[2,2,128,128]{3,2,1,0:T(8,128)(2,1)}) custom-call(s32[16]{0:T(128)} %place_in.1, bf16[32,1024]{1,0:T(8,128)(2,1)} %query_in.1, bf16[128,256]{1,0:T(8,128)(2,1)} %key_in.1, bf16[128,256]{1,0:T(8,128)(2,1)} %value_in.1, bf16[32,1024]{1,0:T(8,128)(2,1)} %saved_in.1, ...), custom_call_target="tpu_custom_call" | custom-call | flops 167772160 | bytes 327680 | tf_op jit(solution)/shard_map/pallas_call | solution.py:301
  24.7 1.7 %shard_map.86 = (bf16[32,1024]{1,0:T(8,128)(2,1)}, bf16[128,256]{1,0:T(8,128)(2,1)}, bf16[128,256]{1,0:T(8,128)(2,1)}) custom-call(bf16[2,8,32,128]{3,2,1,0:T(8,128)(2,1)} %get-tuple-element.6.qpart, bf16[2,2,128,128]{3,2,1,0:T(8,128)(2,1)} %get-tuple-element.7.kpart, bf16[2,2,128,128]{3,2,1,0:T(8,128)(2,1)} %get-tuple-element.8.vpart), custom_call_target="tpu_custom_call" | custom-call | tf_op jit(solution)/shard_map/pallas_call | solution.py:350

commit v5 on v3

v5 whole, which is shorter than its diff:
```python
import functools
import math

import jax
import jax.numpy as jnp
from jax import lax
from jax.experimental import pallas as pl
from jax.experimental.pallas import tpu as pltpu
from jax.sharding import PartitionSpec as P

HEAD_DIM = 128
CORES = 2
DELTA_ROWS = 16
GRANT = 56 * 1024 * 1024
MESH = pl.DeviceIdType.MESH
NT = (((1,), (1,)), ((), ()))
NN = (((1,), (0,)), ((), ()))
TN = (((0,), (0,)), ((), ()))


def matmul(a, b, dims):
    return lax.dot_general(a, b, dims, preferred_element_type=jnp.float32)


def columns(index):
    return pl.ds(pl.multiple_of(index * HEAD_DIM, HEAD_DIM), HEAD_DIM)


def kernel(
    ctx_size, head_size, place_in, query_in, key_in, value_in, saved_in, grad_in,
    dq_out, parts,
    tbuf, kbuf, vbuf, pbuf, dp_stage, dq_stage,
    own_query, own_grad, own_saved, own_key, own_value, token_src, place,
    send_sem, local_sem, t_sem, k_sem, v_sem, p_sem, qp_sem,
):
    chips = ctx_size // CORES
    rows_high = max(chips // 2, 1)
    block = key_in.shape[0]
    token_rows = query_in.shape[0]
    heads = head_size * CORES
    rows = CORES * block
    span = ctx_size * block // place_in.shape[0]
    spans = rows // span
    scale = HEAD_DIM ** -0.5

    me = lax.axis_index("ctx")
    z = lax.axis_index("head")
    core = lax.rem(me, CORES)
    chip = me // CORES
    low, high = lax.rem(chip, 2), chip // 2

    def other_chip(step):
        return lax.rem(high + step // 2, rows_high) * 2 + lax.rem(low + step % 2, 2)

    def other_core(step):
        return lax.rem(core + step, CORES)

    def other_z(step):
        return lax.rem(z + step, head_size)

    chip_at = [other_chip(step) for step in range(chips)]
    core_at = [other_core(step) for step in range(CORES)]
    z_at = [other_z(step) for step in range(head_size)]
    plane = [(c, j) for c in range(chips) for j in range(CORES) if c or j]
    line = [(w, j) for w in range(head_size) for j in range(CORES) if w or j]

    def plane_id(c, j):
        return {"ctx": chip_at[c] * CORES + core_at[j], "head": z}

    def line_id(w, j):
        return {"ctx": chip * CORES + core_at[j], "head": z_at[w]}

    barrier = pltpu.get_barrier_semaphore()
    peers = [plane_id(c, j) for c, j in plane] + [line_id(w, j) for w, j in line if w]
    for peer in peers:
        pl.semaphore_signal(barrier, inc=1, device_id=peer, device_id_type=MESH)

    my_head = z * CORES + core
    held = (
        (grad_in, own_grad), (saved_in, own_saved), (query_in, own_query),
        (key_in, own_key), (value_in, own_value), (place_in, place),
    )
    loads = [pltpu.make_async_copy(src, dst, local_sem.at[i]) for i, (src, dst) in enumerate(held)]
    for load in loads:
        load.start()
    pltpu.make_async_copy(key_in.at[:, columns(core)], kbuf.at[chip, core], k_sem.at[chip, core]).start()
    pltpu.make_async_copy(value_in.at[:, columns(core)], vbuf.at[chip, core], v_sem.at[chip, core]).start()
    for load in loads:
        load.wait()

    product = own_grad[...].astype(jnp.float32) * own_saved[...].astype(jnp.float32)
    coarse = product.astype(jnp.bfloat16)
    fine = (product - coarse.astype(jnp.float32)).astype(jnp.bfloat16)
    shape = (heads, heads * HEAD_DIM)
    member = lax.broadcasted_iota(jnp.int32, shape, 1) // HEAD_DIM == lax.broadcasted_iota(jnp.int32, shape, 0)
    member = jnp.where(member, 1.0, 0.0).astype(jnp.bfloat16)
    delta = matmul(member, jnp.concatenate([coarse] * head_size, axis=0), NT)
    delta += matmul(member, jnp.concatenate([fine] * head_size, axis=0), NT)
    lane_z = lax.broadcasted_iota(jnp.int32, (heads, block), 1) // token_rows
    delta = jnp.where(lane_z == z, delta, 0.0)
    first = delta.astype(jnp.bfloat16).astype(jnp.float32)
    second = (delta - first).astype(jnp.bfloat16).astype(jnp.float32)
    third = delta - first - second
    padding = jnp.zeros((DELTA_ROWS - 3, block), jnp.float32)
    for h in range(heads):
        at = slice(h * HEAD_DIM, (h + 1) * HEAD_DIM)
        token_src[h, :token_rows] = own_query[:, at]
        token_src[h, token_rows : 2 * token_rows] = own_grad[:, at]
        split = jnp.concatenate([first[h : h + 1], second[h : h + 1], third[h : h + 1], padding], axis=0)
        token_src[h, 2 * token_rows :] = split.astype(jnp.bfloat16)
    tbuf[core, z] = token_src[my_head]

    pl.semaphore_wait(barrier, len(peers))

    sent = []

    def send(src, dst, sem, device):
        copy = pltpu.make_async_remote_copy(
            src_ref=src, dst_ref=dst, send_sem=send_sem.at[len(sent)], recv_sem=sem,
            device_id=device, device_id_type=MESH,
        )
        copy.start()
        sent.append(copy)

    def arrive(dst, sem):
        pltpu.make_async_copy(dst, dst, sem).wait()

    def send_plane(src, dst, sem):
        for c, j in plane:
            send(src.at[:, columns(core_at[j])], dst.at[chip, core], sem.at[chip, core], plane_id(c, j))

    for w, j in line:
        send(token_src.at[z_at[w] * CORES + core_at[j]], tbuf.at[core, z], t_sem.at[core, z], line_id(w, j))
    send_plane(own_key, kbuf, k_sem)
    send_plane(own_value, vbuf, v_sem)

    lane = lax.broadcasted_iota(jnp.int32, (1, rows), 1)
    place_row = jnp.zeros((1, rows), jnp.int32)
    for s in range(spans):
        place_row = jnp.where(lane // span == s, place[chip * spans + s], place_row)
    pos_row = place_row * span + lane % span
    within = lax.broadcasted_iota(jnp.int32, (span, rows), 0)

    for w, j in line:
        arrive(tbuf.at[core_at[j], z_at[w]], t_sem.at[core_at[j], z_at[w]])
    query = tbuf[:, :, :token_rows].reshape(rows, HEAD_DIM)
    grad = tbuf[:, :, token_rows : 2 * token_rows].reshape(rows, HEAD_DIM)
    delta_row = jnp.concatenate(
        [
            jnp.sum(
                functools.reduce(
                    jnp.add, [tbuf[j, w, 2 * token_rows :].astype(jnp.float32) for w in range(head_size)]
                ),
                axis=0, keepdims=True,
            )
            for j in range(CORES)
        ],
        axis=1,
    )

    tops, sums = [], []
    for c in range(chips):
        for j in range(CORES):
            arrive(kbuf.at[chip_at[c], j], k_sem.at[chip_at[c], j])
        keys = kbuf[chip_at[c]].reshape(rows, HEAD_DIM)
        scores = matmul(keys, query, NT) * (scale * math.log2(math.e))
        pieces = []
        for s in range(spans):
            limit = pos_row - place[chip_at[c] * spans + s] * span
            pieces.append(jnp.where(within <= limit, scores[s * span : (s + 1) * span], -1e30))
        masked = jnp.concatenate(pieces, axis=0)
        top = jnp.max(masked, axis=0, keepdims=True)
        probs = jnp.exp2(masked - top)
        pbuf[c] = probs
        tops.append(top)
        sums.append(jnp.sum(probs, axis=0, keepdims=True))

    best = functools.reduce(jnp.maximum, tops)
    weights = [jnp.exp2(top - best) for top in tops]
    total = functools.reduce(jnp.add, [w * s for w, s in zip(weights, sums)])
    weights = [w / total for w in weights]

    grad_q = jnp.zeros((rows, HEAD_DIM), jnp.float32)
    for c in range(chips):
        for j in range(CORES):
            arrive(vbuf.at[chip_at[c], j], v_sem.at[chip_at[c], j])
        values = vbuf[chip_at[c]].reshape(rows, HEAD_DIM)
        probs = pbuf[c] * weights[c]
        grad_v = matmul(probs.astype(jnp.bfloat16), grad, NN).astype(jnp.bfloat16)
        dprobs = matmul(values, grad, NT)
        dscores = (probs * (dprobs - delta_row) * scale).astype(jnp.bfloat16)
        grad_k = matmul(dscores, query, NN).astype(jnp.bfloat16)
        for j in range(CORES):
            dp_stage[c, j, 0] = grad_k[j * block : (j + 1) * block]
            dp_stage[c, j, 1] = grad_v[j * block : (j + 1) * block]
        for j in range(CORES):
            src, dst, sem = dp_stage.at[c, core_at[j]], parts.at[chip, core], p_sem.at[chip, core]
            if c or j:
                send(src, dst, sem, plane_id(c, j))
            else:
                pltpu.make_async_copy(src, dst, sem).start()
        grad_q += matmul(dscores, kbuf[chip_at[c]].reshape(rows, HEAD_DIM), TN)

    dq_stage[...] = grad_q.astype(jnp.bfloat16).reshape(dq_stage.shape)
    for w, j in line:
        dst = dq_out.at[:, columns(my_head)]
        send(dq_stage.at[core_at[j], z_at[w]], dst, qp_sem.at[my_head], line_id(w, j))
    own = pltpu.make_async_copy(dq_stage.at[core, z], dq_out.at[:, columns(my_head)], qp_sem.at[my_head])
    own.start()

    for c in range(chips):
        for j in range(CORES):
            arrive(parts.at[c, j], p_sem.at[c, j])
    for h in range(heads):
        arrive(dq_out.at[:, h * HEAD_DIM : (h + 1) * HEAD_DIM], qp_sem.at[h])
    for copy in sent:
        copy.wait_send()


def sum_kernel(dq, parts, dq_out, dk_out, dv_out, dq_buf, buf, dk_buf, dv_buf, load_sem, store_sem):
    chips, cores = parts.shape[:2]
    loads = [pltpu.make_async_copy(parts, buf, load_sem.at[0]), pltpu.make_async_copy(dq, dq_buf, load_sem.at[1])]
    for load in loads:
        load.start()
    loads[0].wait()
    stores = []
    for i, (total, out) in enumerate(((dk_buf, dk_out), (dv_buf, dv_out))):
        for j in range(cores):
            summed = buf[0, j, i].astype(jnp.float32)
            for c in range(1, chips):
                summed += buf[c, j, i].astype(jnp.float32)
            total[:, j * HEAD_DIM : (j + 1) * HEAD_DIM] = summed.astype(jnp.bfloat16)
        stores.append(pltpu.make_async_copy(total, out, store_sem.at[i]))
        stores[-1].start()
    loads[1].wait()
    stores.append(pltpu.make_async_copy(dq_buf, dq_out, store_sem.at[2]))
    stores[-1].start()
    for store in stores:
        store.wait()


def body(query_in, key_in, value_in, out_saved, out_grad, span_place):
    ctx_size, head_size = lax.axis_size("ctx"), lax.axis_size("head")
    chips = ctx_size // CORES
    block = key_in.shape[0]
    token_rows, width = query_in.shape
    heads = head_size * CORES
    rows = CORES * block
    low = jnp.bfloat16
    tokens = (CORES, head_size, token_rows, HEAD_DIM)
    message = (2 * token_rows + DELTA_ROWS, HEAD_DIM)
    keys = (chips, CORES, block, HEAD_DIM)
    pieces = (chips, CORES, 2, block, HEAD_DIM)
    dma = pltpu.SemaphoreType.DMA
    copies = 3 * (ctx_size - 1) + 2 * (heads - 1)
    hbm = pl.BlockSpec(memory_space=pltpu.HBM)
    pairs = CORES * chips * rows * rows
    grads = pl.pallas_call(
        functools.partial(kernel, ctx_size, head_size),
        out_shape=(jax.ShapeDtypeStruct(query_in.shape, low), jax.ShapeDtypeStruct(pieces, low)),
        in_specs=[hbm] * 6,
        out_specs=(hbm, hbm),
        scratch_shapes=[
            pltpu.VMEM((CORES, head_size, *message), low),
            pltpu.VMEM(keys, low),
            pltpu.VMEM(keys, low),
            pltpu.VMEM((chips, rows, rows), jnp.float32),
            pltpu.VMEM(pieces, low),
            pltpu.VMEM(tokens, low),
            pltpu.VMEM((token_rows, width), low),
            pltpu.VMEM((token_rows, width), low),
            pltpu.VMEM((token_rows, width), low),
            pltpu.VMEM(key_in.shape, low),
            pltpu.VMEM(value_in.shape, low),
            pltpu.VMEM((heads, *message), low),
            pltpu.SMEM(span_place.shape, span_place.dtype),
            dma((copies,)),
            dma((6,)),
            dma((CORES, head_size)),
            dma((chips, CORES)),
            dma((chips, CORES)),
            dma((chips, CORES)),
            dma((heads,)),
        ],
        compiler_params=pltpu.CompilerParams(
            collective_id=0, has_side_effects=True, vmem_limit_bytes=GRANT
        ),
        cost_estimate=pl.CostEstimate(
            flops=5 * pairs * HEAD_DIM, bytes_accessed=10 * query_in.size, transcendentals=pairs
        ),
    )(span_place, query_in, key_in, value_in, out_saved, out_grad)
    shapes = (query_in.shape, key_in.shape, value_in.shape)
    return pl.pallas_call(
        sum_kernel,
        out_shape=tuple(jax.ShapeDtypeStruct(shape, low) for shape in shapes),
        in_specs=[hbm] * 2,
        out_specs=(hbm, hbm, hbm),
        scratch_shapes=[
            pltpu.VMEM(query_in.shape, low),
            pltpu.VMEM(pieces, low),
            pltpu.VMEM(key_in.shape, low),
            pltpu.VMEM(value_in.shape, low),
            dma((2,)),
            dma((3,)),
        ],
        compiler_params=pltpu.CompilerParams(vmem_limit_bytes=GRANT),
    )(*grads)


def solution(mesh):
    placed = (
        P(("ctx", "head"), None),
        P("ctx", "head"),
        P("ctx", "head"),
        P(("ctx", "head"), None),
        P(("ctx", "head"), None),
        P(),
    )
    return jax.shard_map(
        body,
        mesh=mesh,
        in_specs=placed,
        out_specs=(P(("ctx", "head"), None), P("ctx", "head"), P("ctx", "head")),
        check_vma=False,
    )
```

time: 23.9 us -> 24.8 us (1.038)
  Pallas kernels: 23.1 us -> 23.9 us
    pallas_call x1, Pallas kernels: 21.3 us -> 22.1 us  [body(): pl.pallas_call(functools.partial(kernel, ctx_size, head_size), out_shape=...]
where the time goes in v5:
time: 24.8 us; the launch traced here: 24.6 us
  Pallas kernels  23.9 us (96%)
  between operations  0.64 us (3%)
    pallas_call x1, Pallas kernels, body(): pl.pallas_call(functools.partial(kernel, ctx_size, head_size), out_shape=...  22.1 us
    pallas_call x1, Pallas kernels, body(): pl.pallas_call(sum_kernel, out_shape=tuple((jax.ShapeDtypeStruct(shape, l...  1.81 us

profile of v5, /device:TPU:0, one launch (start us, length us, event | category | flops | bytes accessed | tf_op | source)
XLA Modules:
  0.0 24.6 jit_solution(6632997757044540290)
XLA Ops:
  0.6 22.1 %shard_map.85 = (bf16[32,1024]{1,0:T(8,128)(2,1)}, bf16[4,2,2,128,128]{4,3,2,1,0:T(8,128)(2,1)}) custom-call(s32[16]{0:T(128)} %place_in.1, bf16[32,1024]{1,0:T(8,128)(2,1)} %query_in.1, bf16[128,256]{1,0:T(8,128)(2,1)} %key_in.1, bf16[128,256]{1,0:T(8,128)(2,1)} %value_in.1, bf16[32,1024]{1,0:T(8,128)(2,1)} %saved_in.1, bf16[32,1024]{1,0:T(8,128)(2,1)} %grad_in.1), custom_call_target="tpu_custom_call" | custom-call | flops 335544320 | bytes 327680 | tf_op jit(solution)/shard_map/pallas_call | solution.py:258
  22.8 1.8 %shard_map.86 = (bf16[32,1024]{1,0:T(8,128)(2,1)}, bf16[128,256]{1,0:T(8,128)(2,1)}, bf16[128,256]{1,0:T(8,128)(2,1)}) custom-call(bf16[32,1024]{1,0:T(8,128)(2,1)} %get-tuple-element.5.dq, bf16[4,2,2,128,128]{4,3,2,1,0:T(8,128)(2,1)} %get-tuple-element.6.parts), custom_call_target="tpu_custom_call" | custom-call | tf_op jit(solution)/shard_map/pallas_call | solution.py:293

commit v6 on v5

--- a/solution.py
+++ b/solution.py
@@ -15,7 +15,6 @@
 MESH = pl.DeviceIdType.MESH
 NT = (((1,), (1,)), ((), ()))
 NN = (((1,), (0,)), ((), ()))
-TN = (((0,), (0,)), ((), ()))
 
 
 def matmul(a, b, dims):
@@ -29,7 +28,7 @@
 def kernel(
     ctx_size, head_size, place_in, query_in, key_in, value_in, saved_in, grad_in,
     dq_out, parts,
-    tbuf, kbuf, vbuf, pbuf, dp_stage, dq_stage,
+    tbuf, kbuf, vbuf, key_cols, pbuf, plow, dslow, dp_stage, dq_stage,
     own_query, own_grad, own_saved, own_key, own_value, token_src, place,
     send_sem, local_sem, t_sem, k_sem, v_sem, p_sem, qp_sem,
 ):
@@ -158,12 +157,20 @@
         axis=1,
     )
 
+    query_cols = query.T
+    grad_cols = grad.T
+
+    def chunk(buf, c):
+        return buf[chip_at[c]].reshape(rows, HEAD_DIM)
+
+    for c in range(chips):
+        for j in range(CORES):
+            arrive(kbuf.at[chip_at[c], j], k_sem.at[chip_at[c], j])
     tops, sums = [], []
     for c in range(chips):
-        for j in range(CORES):
-            arrive(kbuf.at[chip_at[c], j], k_sem.at[chip_at[c], j])
-        keys = kbuf[chip_at[c]].reshape(rows, HEAD_DIM)
-        scores = matmul(keys, query, NT) * (scale * math.log2(math.e))
+        keys = chunk(kbuf, c)
+        key_cols[:, c * rows : (c + 1) * rows] = keys.T
+        scores = matmul(keys, query_cols, NN) * (scale * math.log2(math.e))
         pieces = []
         for s in range(spans):
             limit = pos_row - place[chip_at[c] * spans + s] * span
@@ -180,33 +187,47 @@
     total = functools.reduce(jnp.add, [w * s for w, s in zip(weights, sums)])
     weights = [w / total for w in weights]
 
-    grad_q = jnp.zeros((rows, HEAD_DIM), jnp.float32)
     for c in range(chips):
         for j in range(CORES):
             arrive(vbuf.at[chip_at[c], j], v_sem.at[chip_at[c], j])
-        values = vbuf[chip_at[c]].reshape(rows, HEAD_DIM)
+
+    def score_grads(c):
         probs = pbuf[c] * weights[c]
-        grad_v = matmul(probs.astype(jnp.bfloat16), grad, NN).astype(jnp.bfloat16)
-        dprobs = matmul(values, grad, NT)
-        dscores = (probs * (dprobs - delta_row) * scale).astype(jnp.bfloat16)
-        grad_k = matmul(dscores, query, NN).astype(jnp.bfloat16)
+        plow[c] = probs.astype(jnp.bfloat16)
+        dprobs = matmul(chunk(vbuf, c), grad_cols, NN)
+        dslow[c * rows : (c + 1) * rows] = (probs * (dprobs - delta_row) * scale).astype(jnp.bfloat16)
+
+    def key_grads(c):
+        grad_v = matmul(plow[c], grad, NN).astype(jnp.bfloat16)
+        grad_k = matmul(dslow[c * rows : (c + 1) * rows], query, NN).astype(jnp.bfloat16)
         for j in range(CORES):
             dp_stage[c, j, 0] = grad_k[j * block : (j + 1) * block]
             dp_stage[c, j, 1] = grad_v[j * block : (j + 1) * block]
+
+    def send_key_grads(c):
         for j in range(CORES):
             src, dst, sem = dp_stage.at[c, core_at[j]], parts.at[chip, core], p_sem.at[chip, core]
             if c or j:
                 send(src, dst, sem, plane_id(c, j))
             else:
                 pltpu.make_async_copy(src, dst, sem).start()
-        grad_q += matmul(dscores, kbuf[chip_at[c]].reshape(rows, HEAD_DIM), TN)
-
+
+    order = list(range(chips))[::-1]
+    score_grads(order[0])
+    for now, later in zip(order, order[1:]):
+        key_grads(now)
+        score_grads(later)
+        send_key_grads(now)
+
+    grad_q = matmul(key_cols[...], dslow[...], NN).T
     dq_stage[...] = grad_q.astype(jnp.bfloat16).reshape(dq_stage.shape)
     for w, j in line:
         dst = dq_out.at[:, columns(my_head)]
         send(dq_stage.at[core_at[j], z_at[w]], dst, qp_sem.at[my_head], line_id(w, j))
     own = pltpu.make_async_copy(dq_stage.at[core, z], dq_out.at[:, columns(my_head)], qp_sem.at[my_head])
     own.start()
+    key_grads(0)
+    send_key_grads(0)
 
     for c in range(chips):
         for j in range(CORES):
@@ -264,7 +285,10 @@
             pltpu.VMEM((CORES, head_size, *message), low),
             pltpu.VMEM(keys, low),
             pltpu.VMEM(keys, low),
+            pltpu.VMEM((HEAD_DIM, chips * rows), low),
             pltpu.VMEM((chips, rows, rows), jnp.float32),
+            pltpu.VMEM((chips, rows, rows), low),
+            pltpu.VMEM((chips * rows, rows), low),
             pltpu.VMEM(pieces, low),
             pltpu.VMEM(tokens, low),
             pltpu.VMEM((token_rows, width), low),

time: 24.8 us -> 24.9 us (level)
  no operation moved by 1% of the time
where the time goes in v6:
time: 24.9 us; the launch traced here: 24.7 us
  Pallas kernels  24 us (96%)
  between operations  0.64 us (3%)
    pallas_call x1, Pallas kernels, body(): pl.pallas_call(functools.partial(kernel, ctx_size, head_size), out_shape=...  22.2 us
    pallas_call x1, Pallas kernels, body(): pl.pallas_call(sum_kernel, out_shape=tuple((jax.ShapeDtypeStruct(shape, l...  1.81 us

profile of v6, /device:TPU:0, one launch (start us, length us, event | category | flops | bytes accessed | tf_op | source)
XLA Modules:
  0.0 24.7 jit_solution(17002236343407135289)
XLA Ops:
  0.6 22.2 %shard_map.85 = (bf16[32,1024]{1,0:T(8,128)(2,1)}, bf16[4,2,2,128,128]{4,3,2,1,0:T(8,128)(2,1)}) custom-call(s32[16]{0:T(128)} %place_in.1, bf16[32,1024]{1,0:T(8,128)(2,1)} %query_in.1, bf16[128,256]{1,0:T(8,128)(2,1)} %key_in.1, bf16[128,256]{1,0:T(8,128)(2,1)} %value_in.1, bf16[32,1024]{1,0:T(8,128)(2,1)} %saved_in.1, bf16[32,1024]{1,0:T(8,128)(2,1)} %grad_in.1), custom_call_target="tpu_custom_call" | custom-call | flops 335544320 | bytes 327680 | tf_op jit(solution)/shard_map/pallas_call | solution.py:279
  22.9 1.8 %shard_map.86 = (bf16[32,1024]{1,0:T(8,128)(2,1)}, bf16[128,256]{1,0:T(8,128)(2,1)}, bf16[128,256]{1,0:T(8,128)(2,1)}) custom-call(bf16[32,1024]{1,0:T(8,128)(2,1)} %get-tuple-element.5.dq, bf16[4,2,2,128,128]{4,3,2,1,0:T(8,128)(2,1)} %get-tuple-element.6.parts), custom_call_target="tpu_custom_call" | custom-call | tf_op jit(solution)/shard_map/pallas_call | solution.py:317

commit v7 on v5

--- a/solution.py
+++ b/solution.py
@@ -15,7 +15,6 @@
 MESH = pl.DeviceIdType.MESH
 NT = (((1,), (1,)), ((), ()))
 NN = (((1,), (0,)), ((), ()))
-TN = (((0,), (0,)), ((), ()))
 
 
 def matmul(a, b, dims):
@@ -29,7 +28,7 @@
 def kernel(
     ctx_size, head_size, place_in, query_in, key_in, value_in, saved_in, grad_in,
     dq_out, parts,
-    tbuf, kbuf, vbuf, pbuf, dp_stage, dq_stage,
+    tbuf, kbuf, vbuf, key_cols, pbuf, dp_stage, dq_stage,
     own_query, own_grad, own_saved, own_key, own_value, token_src, place,
     send_sem, local_sem, t_sem, k_sem, v_sem, p_sem, qp_sem,
 ):
@@ -126,7 +125,7 @@
         pltpu.make_async_copy(dst, dst, sem).wait()
 
     def send_plane(src, dst, sem):
-        for c, j in plane:
+        for c, j in plane[::-1]:
             send(src.at[:, columns(core_at[j])], dst.at[chip, core], sem.at[chip, core], plane_id(c, j))
 
     for w, j in line:
@@ -158,12 +157,19 @@
         axis=1,
     )
 
+    query_cols = query.T
+    grad_cols = grad.T
+
+    def chunk(buf, c):
+        return buf[chip_at[c]].reshape(rows, HEAD_DIM)
+
     tops, sums = [], []
     for c in range(chips):
         for j in range(CORES):
             arrive(kbuf.at[chip_at[c], j], k_sem.at[chip_at[c], j])
-        keys = kbuf[chip_at[c]].reshape(rows, HEAD_DIM)
-        scores = matmul(keys, query, NT) * (scale * math.log2(math.e))
+        keys = chunk(kbuf, c)
+        key_cols[:, c * rows : (c + 1) * rows] = keys.T
+        scores = matmul(keys, query_cols, NN) * (scale * math.log2(math.e))
         pieces = []
         for s in range(spans):
             limit = pos_row - place[chip_at[c] * spans + s] * span
@@ -180,26 +186,32 @@
     total = functools.reduce(jnp.add, [w * s for w, s in zip(weights, sums)])
     weights = [w / total for w in weights]
 
-    grad_q = jnp.zeros((rows, HEAD_DIM), jnp.float32)
-    for c in range(chips):
+    def send_part(c, kind, total):
+        total = total.astype(jnp.bfloat16)
+        for j in range(CORES):
+            dp_stage[c, j, kind] = total[j * block : (j + 1) * block]
+        for j in range(CORES):
+            src, dst = dp_stage.at[c, core_at[j], kind], parts.at[chip, core, kind]
+            if c or j:
+                send(src, dst, p_sem.at[kind, chip, core], plane_id(c, j))
+            else:
+                pltpu.make_async_copy(src, dst, p_sem.at[kind, chip, core]).start()
+
+    far_first = list(range(chips))[::-1]
+    for c in far_first:
+        probs = pbuf[c] * weights[c]
+        pbuf[c] = probs
+        send_part(c, 1, matmul(probs.astype(jnp.bfloat16), grad, NN))
+
+    grad_q = jnp.zeros((HEAD_DIM, rows), jnp.float32)
+    for c in far_first[-1:] + far_first[:-1]:
         for j in range(CORES):
             arrive(vbuf.at[chip_at[c], j], v_sem.at[chip_at[c], j])
-        values = vbuf[chip_at[c]].reshape(rows, HEAD_DIM)
-        probs = pbuf[c] * weights[c]
-        grad_v = matmul(probs.astype(jnp.bfloat16), grad, NN).astype(jnp.bfloat16)
-        dprobs = matmul(values, grad, NT)
-        dscores = (probs * (dprobs - delta_row) * scale).astype(jnp.bfloat16)
-        grad_k = matmul(dscores, query, NN).astype(jnp.bfloat16)
-        for j in range(CORES):
-            dp_stage[c, j, 0] = grad_k[j * block : (j + 1) * block]
-            dp_stage[c, j, 1] = grad_v[j * block : (j + 1) * block]
-        for j in range(CORES):
-            src, dst, sem = dp_stage.at[c, core_at[j]], parts.at[chip, core], p_sem.at[chip, core]
-            if c or j:
-                send(src, dst, sem, plane_id(c, j))
-            else:
-                pltpu.make_async_copy(src, dst, sem).start()
-        grad_q += matmul(dscores, kbuf[chip_at[c]].reshape(rows, HEAD_DIM), TN)
+        dprobs = matmul(chunk(vbuf, c), grad_cols, NN)
+        dscores = (pbuf[c] * (dprobs - delta_row) * scale).astype(jnp.bfloat16)
+        send_part(c, 0, matmul(dscores, query, NN))
+        grad_q += matmul(key_cols[:, c * rows : (c + 1) * rows], dscores, NN)
+    grad_q = grad_q.T
 
     dq_stage[...] = grad_q.astype(jnp.bfloat16).reshape(dq_stage.shape)
     for w, j in line:
@@ -210,7 +222,8 @@
 
     for c in range(chips):
         for j in range(CORES):
-            arrive(parts.at[c, j], p_sem.at[c, j])
+            for kind in range(2):
+                arrive(parts.at[c, j, kind], p_sem.at[kind, c, j])
     for h in range(heads):
         arrive(dq_out.at[:, h * HEAD_DIM : (h + 1) * HEAD_DIM], qp_sem.at[h])
     for copy in sent:
@@ -252,7 +265,7 @@
     keys = (chips, CORES, block, HEAD_DIM)
     pieces = (chips, CORES, 2, block, HEAD_DIM)
     dma = pltpu.SemaphoreType.DMA
-    copies = 3 * (ctx_size - 1) + 2 * (heads - 1)
+    copies = 4 * (ctx_size - 1) + 2 * (heads - 1)
     hbm = pl.BlockSpec(memory_space=pltpu.HBM)
     pairs = CORES * chips * rows * rows
     grads = pl.pallas_call(
@@ -264,6 +277,7 @@
             pltpu.VMEM((CORES, head_size, *message), low),
             pltpu.VMEM(keys, low),
             pltpu.VMEM(keys, low),
+            pltpu.VMEM((HEAD_DIM, chips * rows), low),
             pltpu.VMEM((chips, rows, rows), jnp.float32),
             pltpu.VMEM(pieces, low),
             pltpu.VMEM(tokens, low),
@@ -279,7 +293,7 @@
             dma((CORES, head_size)),
             dma((chips, CORES)),
             dma((chips, CORES)),
-            dma((chips, CORES)),
+            dma((2, chips, CORES)),
             dma((heads,)),
         ],
         compiler_params=pltpu.CompilerParams(

time: 24.8 us -> 23.1 us (0.931)
  Pallas kernels: 23.9 us -> 22.2 us
    pallas_call x1, Pallas kernels: 22.1 us -> 20.4 us  [body(): pl.pallas_call(functools.partial(kernel, ctx_size, head_size), out_shape=...]
where the time goes in v7:
time: 23.1 us; the launch traced here: 22.9 us
  Pallas kernels  22.2 us (96%)
  between operations  0.64 us (3%)
    pallas_call x1, Pallas kernels, body(): pl.pallas_call(functools.partial(kernel, ctx_size, head_size), out_shape=...  20.4 us
    pallas_call x1, Pallas kernels, body(): pl.pallas_call(sum_kernel, out_shape=tuple((jax.ShapeDtypeStruct(shape, l...  1.81 us

profile of v7, /device:TPU:0, one launch (start us, length us, event | category | flops | bytes accessed | tf_op | source)
XLA Modules:
  0.0 22.9 jit_solution(551677641784860695)
XLA Ops:
  0.6 20.4 %shard_map.85 = (bf16[32,1024]{1,0:T(8,128)(2,1)}, bf16[4,2,2,128,128]{4,3,2,1,0:T(8,128)(2,1)}) custom-call(s32[16]{0:T(128)} %place_in.1, bf16[32,1024]{1,0:T(8,128)(2,1)} %query_in.1, bf16[128,256]{1,0:T(8,128)(2,1)} %key_in.1, bf16[128,256]{1,0:T(8,128)(2,1)} %value_in.1, bf16[32,1024]{1,0:T(8,128)(2,1)} %saved_in.1, bf16[32,1024]{1,0:T(8,128)(2,1)} %grad_in.1), custom_call_target="tpu_custom_call" | custom-call | flops 335544320 | bytes 327680 | tf_op jit(solution)/shard_map/pallas_call | solution.py:271
  21.1 1.8 %shard_map.86 = (bf16[32,1024]{1,0:T(8,128)(2,1)}, bf16[128,256]{1,0:T(8,128)(2,1)}, bf16[128,256]{1,0:T(8,128)(2,1)}) custom-call(bf16[32,1024]{1,0:T(8,128)(2,1)} %get-tuple-element.5.dq, bf16[4,2,2,128,128]{4,3,2,1,0:T(8,128)(2,1)} %get-tuple-element.6.parts), custom_call_target="tpu_custom_call" | custom-call | tf_op jit(solution)/shard_map/pallas_call | solution.py:307

commit v8 on v7

--- a/solution.py
+++ b/solution.py
@@ -28,9 +28,9 @@
 def kernel(
     ctx_size, head_size, place_in, query_in, key_in, value_in, saved_in, grad_in,
     dq_out, parts,
-    tbuf, kbuf, vbuf, key_cols, pbuf, dp_stage, dq_stage,
-    own_query, own_grad, own_saved, own_key, own_value, token_src, place,
-    send_sem, local_sem, t_sem, k_sem, v_sem, p_sem, qp_sem,
+    qbuf, tbuf, kbuf, vbuf, key_cols, pbuf, dp_stage, dq_stage,
+    own_grad, own_saved, token_src, place,
+    send_sem, local_sem, q_sem, t_sem, k_sem, v_sem, p_sem, qp_sem,
 ):
     chips = ctx_size // CORES
     rows_high = max(chips // 2, 1)
@@ -75,18 +75,41 @@
         pl.semaphore_signal(barrier, inc=1, device_id=peer, device_id_type=MESH)
 
     my_head = z * CORES + core
-    held = (
-        (grad_in, own_grad), (saved_in, own_saved), (query_in, own_query),
-        (key_in, own_key), (value_in, own_value), (place_in, place),
-    )
+    held = ((grad_in, own_grad), (saved_in, own_saved), (place_in, place))
     loads = [pltpu.make_async_copy(src, dst, local_sem.at[i]) for i, (src, dst) in enumerate(held)]
     for load in loads:
         load.start()
+    pltpu.make_async_copy(query_in.at[:, columns(my_head)], qbuf.at[core, z], q_sem.at[core, z]).start()
     pltpu.make_async_copy(key_in.at[:, columns(core)], kbuf.at[chip, core], k_sem.at[chip, core]).start()
     pltpu.make_async_copy(value_in.at[:, columns(core)], vbuf.at[chip, core], v_sem.at[chip, core]).start()
+
+    pl.semaphore_wait(barrier, len(peers))
+
+    sent = []
+
+    def send(src, dst, sem, device):
+        copy = pltpu.make_async_remote_copy(
+            src_ref=src, dst_ref=dst, send_sem=send_sem.at[len(sent)], recv_sem=sem,
+            device_id=device, device_id_type=MESH,
+        )
+        copy.start()
+        sent.append(copy)
+
+    def arrive(dst, sem):
+        pltpu.make_async_copy(dst, dst, sem).wait()
+
+    def send_plane(src, dst, sem):
+        for c, j in plane[::-1]:
+            send(src.at[:, columns(core_at[j])], dst.at[chip, core], sem.at[chip, core], plane_id(c, j))
+
+    for w, j in line:
+        src = query_in.at[:, columns(z_at[w] * CORES + core_at[j])]
+        send(src, qbuf.at[core, z], q_sem.at[core, z], line_id(w, j))
+    send_plane(key_in, kbuf, k_sem)
+    send_plane(value_in, vbuf, v_sem)
+
     for load in loads:
         load.wait()
-
     product = own_grad[...].astype(jnp.float32) * own_saved[...].astype(jnp.float32)
     coarse = product.astype(jnp.bfloat16)
     fine = (product - coarse.astype(jnp.float32)).astype(jnp.bfloat16)
@@ -103,35 +126,13 @@
     padding = jnp.zeros((DELTA_ROWS - 3, block), jnp.float32)
     for h in range(heads):
         at = slice(h * HEAD_DIM, (h + 1) * HEAD_DIM)
-        token_src[h, :token_rows] = own_query[:, at]
-        token_src[h, token_rows : 2 * token_rows] = own_grad[:, at]
+        token_src[h, :token_rows] = own_grad[:, at]
         split = jnp.concatenate([first[h : h + 1], second[h : h + 1], third[h : h + 1], padding], axis=0)
-        token_src[h, 2 * token_rows :] = split.astype(jnp.bfloat16)
+        token_src[h, token_rows:] = split.astype(jnp.bfloat16)
     tbuf[core, z] = token_src[my_head]
-
-    pl.semaphore_wait(barrier, len(peers))
-
-    sent = []
-
-    def send(src, dst, sem, device):
-        copy = pltpu.make_async_remote_copy(
-            src_ref=src, dst_ref=dst, send_sem=send_sem.at[len(sent)], recv_sem=sem,
-            device_id=device, device_id_type=MESH,
-        )
-        copy.start()
-        sent.append(copy)
-
-    def arrive(dst, sem):
-        pltpu.make_async_copy(dst, dst, sem).wait()
-
-    def send_plane(src, dst, sem):
-        for c, j in plane[::-1]:
-            send(src.at[:, columns(core_at[j])], dst.at[chip, core], sem.at[chip, core], plane_id(c, j))
 
     for w, j in line:
         send(token_src.at[z_at[w] * CORES + core_at[j]], tbuf.at[core, z], t_sem.at[core, z], line_id(w, j))
-    send_plane(own_key, kbuf, k_sem)
-    send_plane(own_value, vbuf, v_sem)
 
     lane = lax.broadcasted_iota(jnp.int32, (1, rows), 1)
     place_row = jnp.zeros((1, rows), jnp.int32)
@@ -140,25 +141,11 @@
     pos_row = place_row * span + lane % span
     within = lax.broadcasted_iota(jnp.int32, (span, rows), 0)
 
-    for w, j in line:
-        arrive(tbuf.at[core_at[j], z_at[w]], t_sem.at[core_at[j], z_at[w]])
-    query = tbuf[:, :, :token_rows].reshape(rows, HEAD_DIM)
-    grad = tbuf[:, :, token_rows : 2 * token_rows].reshape(rows, HEAD_DIM)
-    delta_row = jnp.concatenate(
-        [
-            jnp.sum(
-                functools.reduce(
-                    jnp.add, [tbuf[j, w, 2 * token_rows :].astype(jnp.float32) for w in range(head_size)]
-                ),
-                axis=0, keepdims=True,
-            )
-            for j in range(CORES)
-        ],
-        axis=1,
-    )
-
+    for j in range(CORES):
+        for w in range(head_size):
+            arrive(qbuf.at[j, w], q_sem.at[j, w])
+    query = qbuf[...].reshape(rows, HEAD_DIM)
     query_cols = query.T
-    grad_cols = grad.T
 
     def chunk(buf, c):
         return buf[chip_at[c]].reshape(rows, HEAD_DIM)
@@ -185,6 +172,24 @@
     weights = [jnp.exp2(top - best) for top in tops]
     total = functools.reduce(jnp.add, [w * s for w, s in zip(weights, sums)])
     weights = [w / total for w in weights]
+
+    for w, j in line:
+        arrive(tbuf.at[core_at[j], z_at[w]], t_sem.at[core_at[j], z_at[w]])
+    grad = tbuf[:, :, :token_rows].reshape(rows, HEAD_DIM)
+    delta_row = jnp.concatenate(
+        [
+            jnp.sum(
+                functools.reduce(
+                    jnp.add, [tbuf[j, w, token_rows :].astype(jnp.float32) for w in range(head_size)]
+                ),
+                axis=0, keepdims=True,
+            )
+            for j in range(CORES)
+        ],
+        axis=1,
+    )
+
+    grad_cols = grad.T
 
     def send_part(c, kind, total):
         total = total.astype(jnp.bfloat16)
@@ -261,11 +266,11 @@
     rows = CORES * block
     low = jnp.bfloat16
     tokens = (CORES, head_size, token_rows, HEAD_DIM)
-    message = (2 * token_rows + DELTA_ROWS, HEAD_DIM)
+    message = (token_rows + DELTA_ROWS, HEAD_DIM)
     keys = (chips, CORES, block, HEAD_DIM)
     pieces = (chips, CORES, 2, block, HEAD_DIM)
     dma = pltpu.SemaphoreType.DMA
-    copies = 4 * (ctx_size - 1) + 2 * (heads - 1)
+    copies = 4 * (ctx_size - 1) + 3 * (heads - 1)
     hbm = pl.BlockSpec(memory_space=pltpu.HBM)
     pairs = CORES * chips * rows * rows
     grads = pl.pallas_call(
@@ -274,6 +279,7 @@
         in_specs=[hbm] * 6,
         out_specs=(hbm, hbm),
         scratch_shapes=[
+            pltpu.VMEM(tokens, low),
             pltpu.VMEM((CORES, head_size, *message), low),
             pltpu.VMEM(keys, low),
             pltpu.VMEM(keys, low),
@@ -283,13 +289,11 @@
             pltpu.VMEM(tokens, low),
             pltpu.VMEM((token_rows, width), low),
             pltpu.VMEM((token_rows, width), low),
-            pltpu.VMEM((token_rows, width), low),
-            pltpu.VMEM(key_in.shape, low),
-            pltpu.VMEM(value_in.shape, low),
             pltpu.VMEM((heads, *message), low),
             pltpu.SMEM(span_place.shape, span_place.dtype),
             dma((copies,)),
-            dma((6,)),
+            dma((3,)),
+            dma((CORES, head_size)),
             dma((CORES, head_size)),
             dma((chips, CORES)),
             dma((chips, CORES)),

time: 23.1 us -> 23.4 us (1.013)
  Pallas kernels: 22.2 us -> 22.6 us
    pallas_call x1, Pallas kernels: 20.4 us -> 20.8 us  [body(): pl.pallas_call(functools.partial(kernel, ctx_size, head_size), out_shape=...]
where the time goes in v8:
time: 23.4 us; the launch traced here: 23.2 us
  Pallas kernels  22.6 us (97%)
  between operations  0.64 us (3%)
    pallas_call x1, Pallas kernels, body(): pl.pallas_call(functools.partial(kernel, ctx_size, head_size), out_shape=...  20.8 us
    pallas_call x1, Pallas kernels, body(): pl.pallas_call(sum_kernel, out_shape=tuple((jax.ShapeDtypeStruct(shape, l...  1.81 us

profile of v8, /device:TPU:0, one launch (start us, length us, event | category | flops | bytes accessed | tf_op | source)
XLA Modules:
  0.0 23.2 jit_solution(14130856144179960549)
XLA Ops:
  0.6 20.8 %shard_map.85 = (bf16[32,1024]{1,0:T(8,128)(2,1)}, bf16[4,2,2,128,128]{4,3,2,1,0:T(8,128)(2,1)}) custom-call(s32[16]{0:T(128)} %place_in.1, bf16[32,1024]{1,0:T(8,128)(2,1)} %query_in.1, bf16[128,256]{1,0:T(8,128)(2,1)} %key_in.1, bf16[128,256]{1,0:T(8,128)(2,1)} %value_in.1, bf16[32,1024]{1,0:T(8,128)(2,1)} %saved_in.1, bf16[32,1024]{1,0:T(8,128)(2,1)} %grad_in.1), custom_call_target="tpu_custom_call" | custom-call | flops 335544320 | bytes 327680 | tf_op jit(solution)/shard_map/pallas_call | solution.py:276
  21.4 1.8 %shard_map.86 = (bf16[32,1024]{1,0:T(8,128)(2,1)}, bf16[128,256]{1,0:T(8,128)(2,1)}, bf16[128,256]{1,0:T(8,128)(2,1)}) custom-call(bf16[32,1024]{1,0:T(8,128)(2,1)} %get-tuple-element.5.dq, bf16[4,2,2,128,128]{4,3,2,1,0:T(8,128)(2,1)} %get-tuple-element.6.parts), custom_call_target="tpu_custom_call" | custom-call | tf_op jit(solution)/shard_map/pallas_call | solution.py:311

commit v9 on v8

--- a/solution.py
+++ b/solution.py
@@ -12,6 +12,7 @@
 CORES = 2
 DELTA_ROWS = 16
 GRANT = 56 * 1024 * 1024
+SMALL_GRANT = 8 * 1024 * 1024
 MESH = pl.DeviceIdType.MESH
 NT = (((1,), (1,)), ((), ()))
 NN = (((1,), (0,)), ((), ()))
@@ -235,24 +236,18 @@
         copy.wait_send()
 
 
-def sum_kernel(dq, parts, dq_out, dk_out, dv_out, dq_buf, buf, dk_buf, dv_buf, load_sem, store_sem):
+def sum_kernel(dq, parts, dq_out, dk_out, dv_out, dk_buf, dv_buf, store_sem):
     chips, cores = parts.shape[:2]
-    loads = [pltpu.make_async_copy(parts, buf, load_sem.at[0]), pltpu.make_async_copy(dq, dq_buf, load_sem.at[1])]
-    for load in loads:
-        load.start()
-    loads[0].wait()
-    stores = []
+    stores = [pltpu.make_async_copy(dq, dq_out, store_sem.at[2])]
+    stores[0].start()
     for i, (total, out) in enumerate(((dk_buf, dk_out), (dv_buf, dv_out))):
         for j in range(cores):
-            summed = buf[0, j, i].astype(jnp.float32)
+            summed = parts[0, j, i].astype(jnp.float32)
             for c in range(1, chips):
-                summed += buf[c, j, i].astype(jnp.float32)
+                summed += parts[c, j, i].astype(jnp.float32)
             total[:, j * HEAD_DIM : (j + 1) * HEAD_DIM] = summed.astype(jnp.bfloat16)
         stores.append(pltpu.make_async_copy(total, out, store_sem.at[i]))
         stores[-1].start()
-    loads[1].wait()
-    stores.append(pltpu.make_async_copy(dq_buf, dq_out, store_sem.at[2]))
-    stores[-1].start()
     for store in stores:
         store.wait()
 
@@ -272,12 +267,13 @@
     dma = pltpu.SemaphoreType.DMA
     copies = 4 * (ctx_size - 1) + 3 * (heads - 1)
     hbm = pl.BlockSpec(memory_space=pltpu.HBM)
+    vmem = pl.BlockSpec(memory_space=pltpu.VMEM)
     pairs = CORES * chips * rows * rows
     grads = pl.pallas_call(
         functools.partial(kernel, ctx_size, head_size),
-        out_shape=(jax.ShapeDtypeStruct(query_in.shape, low), jax.ShapeDtypeStruct(pieces, low)),
+        out_shape=(pltpu.VMEM(query_in.shape, low), pltpu.VMEM(pieces, low)),
         in_specs=[hbm] * 6,
-        out_specs=(hbm, hbm),
+        out_specs=(vmem, vmem),
         scratch_shapes=[
             pltpu.VMEM(tokens, low),
             pltpu.VMEM((CORES, head_size, *message), low),
@@ -311,17 +307,14 @@
     return pl.pallas_call(
         sum_kernel,
         out_shape=tuple(jax.ShapeDtypeStruct(shape, low) for shape in shapes),
-        in_specs=[hbm] * 2,
+        in_specs=[vmem] * 2,
         out_specs=(hbm, hbm, hbm),
         scratch_shapes=[
-            pltpu.VMEM(query_in.shape, low),
-            pltpu.VMEM(pieces, low),
             pltpu.VMEM(key_in.shape, low),
             pltpu.VMEM(value_in.shape, low),
-            dma((2,)),
             dma((3,)),
         ],
-        compiler_params=pltpu.CompilerParams(vmem_limit_bytes=GRANT),
+        compiler_params=pltpu.CompilerParams(vmem_limit_bytes=SMALL_GRANT),
     )(*grads)
 
 

time: 23.4 us -> 22.2 us (0.949)
  Pallas kernels: 22.6 us -> 21.4 us
    pallas_call x1, Pallas kernels: 1.81 us -> 0.73 us  [body(): pl.pallas_call(sum_kernel, out_shape=tuple((jax.ShapeDtypeStruct(shape, l...]
where the time goes in v9:
time: 22.2 us; the launch traced here: 22 us
  Pallas kernels  21.4 us (96%)
  between operations  0.64 us (3%)
    pallas_call x1, Pallas kernels, body(): pl.pallas_call(functools.partial(kernel, ctx_size, head_size), out_shape=...  20.7 us
    pallas_call x1, Pallas kernels, body(): pl.pallas_call(sum_kernel, out_shape=tuple((jax.ShapeDtypeStruct(shape, l...  0.73 us

profile of v9, /device:TPU:0, one launch (start us, length us, event | category | flops | bytes accessed | tf_op | source)
XLA Modules:
  0.0 22.0 jit_solution(607409639360380245)
XLA Ops:
  0.6 20.7 %shard_map.85 = (bf16[32,1024]{1,0:T(8,128)(2,1)S(1)}, bf16[4,2,2,128,128]{4,3,2,1,0:T(8,128)(2,1)S(1)}) custom-call(s32[16]{0:T(128)} %place_in.1, bf16[32,1024]{1,0:T(8,128)(2,1)} %query_in.1, bf16[128,256]{1,0:T(8,128)(2,1)} %key_in.1, bf16[128,256]{1,0:T(8,128)(2,1)} %value_in.1, bf16[32,1024]{1,0:T(8,128)(2,1)} %saved_in.1, bf16[32,1024]{1,0:T(8,128)(2,1)} %grad_in.1), custom_call_target="tpu_custom_call" | custom-call | flops 335544320 | bytes 327680 | tf_op jit(solution)/shard_map/pallas_call | solution.py:272
  21.3 0.7 %shard_map.86 = (bf16[32,1024]{1,0:T(8,128)(2,1)}, bf16[128,256]{1,0:T(8,128)(2,1)}, bf16[128,256]{1,0:T(8,128)(2,1)}) custom-call(bf16[32,1024]{1,0:T(8,128)(2,1)S(1)} %get-tuple-element.5.dq, bf16[4,2,2,128,128]{4,3,2,1,0:T(8,128)(2,1)S(1)} %get-tuple-element.6.parts), custom_call_target="tpu_custom_call" | custom-call | tf_op jit(solution)/shard_map/pallas_call | solution.py:307

commit v10 on v9

--- a/solution.py
+++ b/solution.py
@@ -80,9 +80,9 @@
     loads = [pltpu.make_async_copy(src, dst, local_sem.at[i]) for i, (src, dst) in enumerate(held)]
     for load in loads:
         load.start()
-    pltpu.make_async_copy(query_in.at[:, columns(my_head)], qbuf.at[core, z], q_sem.at[core, z]).start()
-    pltpu.make_async_copy(key_in.at[:, columns(core)], kbuf.at[chip, core], k_sem.at[chip, core]).start()
-    pltpu.make_async_copy(value_in.at[:, columns(core)], vbuf.at[chip, core], v_sem.at[chip, core]).start()
+    pltpu.make_async_copy(query_in.at[:, columns(my_head)], qbuf.at[core, z], q_sem.at[0]).start()
+    pltpu.make_async_copy(key_in.at[:, columns(core)], kbuf.at[chip, core], k_sem.at[chip]).start()
+    pltpu.make_async_copy(value_in.at[:, columns(core)], vbuf.at[chip, core], v_sem.at[chip]).start()
 
     pl.semaphore_wait(barrier, len(peers))
 
@@ -101,13 +101,12 @@
 
     def send_plane(src, dst, sem):
         for c, j in plane[::-1]:
-            send(src.at[:, columns(core_at[j])], dst.at[chip, core], sem.at[chip, core], plane_id(c, j))
+            send(src.at[:, columns(core_at[j])], dst.at[chip, core], sem.at[chip], plane_id(c, j))
 
     for w, j in line:
         src = query_in.at[:, columns(z_at[w] * CORES + core_at[j])]
-        send(src, qbuf.at[core, z], q_sem.at[core, z], line_id(w, j))
+        send(src, qbuf.at[core, z], q_sem.at[0], line_id(w, j))
     send_plane(key_in, kbuf, k_sem)
-    send_plane(value_in, vbuf, v_sem)
 
     for load in loads:
         load.wait()
@@ -130,10 +129,11 @@
         token_src[h, :token_rows] = own_grad[:, at]
         split = jnp.concatenate([first[h : h + 1], second[h : h + 1], third[h : h + 1], padding], axis=0)
         token_src[h, token_rows:] = split.astype(jnp.bfloat16)
-    tbuf[core, z] = token_src[my_head]
+    pltpu.make_async_copy(token_src.at[my_head], tbuf.at[core, z], t_sem.at[0]).start()
 
     for w, j in line:
-        send(token_src.at[z_at[w] * CORES + core_at[j]], tbuf.at[core, z], t_sem.at[core, z], line_id(w, j))
+        send(token_src.at[z_at[w] * CORES + core_at[j]], tbuf.at[core, z], t_sem.at[0], line_id(w, j))
+    send_plane(value_in, vbuf, v_sem)
 
     lane = lax.broadcasted_iota(jnp.int32, (1, rows), 1)
     place_row = jnp.zeros((1, rows), jnp.int32)
@@ -142,9 +142,7 @@
     pos_row = place_row * span + lane % span
     within = lax.broadcasted_iota(jnp.int32, (span, rows), 0)
 
-    for j in range(CORES):
-        for w in range(head_size):
-            arrive(qbuf.at[j, w], q_sem.at[j, w])
+    arrive(qbuf, q_sem.at[0])
     query = qbuf[...].reshape(rows, HEAD_DIM)
     query_cols = query.T
 
@@ -153,8 +151,7 @@
 
     tops, sums = [], []
     for c in range(chips):
-        for j in range(CORES):
-            arrive(kbuf.at[chip_at[c], j], k_sem.at[chip_at[c], j])
+        arrive(kbuf.at[chip_at[c]], k_sem.at[chip_at[c]])
         keys = chunk(kbuf, c)
         key_cols[:, c * rows : (c + 1) * rows] = keys.T
         scores = matmul(keys, query_cols, NN) * (scale * math.log2(math.e))
@@ -174,8 +171,7 @@
     total = functools.reduce(jnp.add, [w * s for w, s in zip(weights, sums)])
     weights = [w / total for w in weights]
 
-    for w, j in line:
-        arrive(tbuf.at[core_at[j], z_at[w]], t_sem.at[core_at[j], z_at[w]])
+    arrive(tbuf, t_sem.at[0])
     grad = tbuf[:, :, :token_rows].reshape(rows, HEAD_DIM)
     delta_row = jnp.concatenate(
         [
@@ -199,9 +195,9 @@
         for j in range(CORES):
             src, dst = dp_stage.at[c, core_at[j], kind], parts.at[chip, core, kind]
             if c or j:
-                send(src, dst, p_sem.at[kind, chip, core], plane_id(c, j))
+                send(src, dst, p_sem.at[0], plane_id(c, j))
             else:
-                pltpu.make_async_copy(src, dst, p_sem.at[kind, chip, core]).start()
+                pltpu.make_async_copy(src, dst, p_sem.at[0]).start()
 
     far_first = list(range(chips))[::-1]
     for c in far_first:
@@ -210,30 +206,25 @@
         send_part(c, 1, matmul(probs.astype(jnp.bfloat16), grad, NN))
 
     grad_q = jnp.zeros((HEAD_DIM, rows), jnp.float32)
-    for c in far_first[-1:] + far_first[:-1]:
-        for j in range(CORES):
-            arrive(vbuf.at[chip_at[c], j], v_sem.at[chip_at[c], j])
+    order = far_first[-1:] + far_first[:-1]
+    last = order[-1]
+    for c in order:
+        arrive(vbuf.at[chip_at[c]], v_sem.at[chip_at[c]])
         dprobs = matmul(chunk(vbuf, c), grad_cols, NN)
         dscores = (pbuf[c] * (dprobs - delta_row) * scale).astype(jnp.bfloat16)
+        grad_q += matmul(key_cols[:, c * rows : (c + 1) * rows], dscores, NN)
+        if c == last:
+            dq_stage[...] = grad_q.T.astype(jnp.bfloat16).reshape(dq_stage.shape)
+            dst = dq_out.at[:, columns(my_head)]
+            for w, j in line:
+                send(dq_stage.at[core_at[j], z_at[w]], dst, qp_sem.at[0], line_id(w, j))
+            pltpu.make_async_copy(dq_stage.at[core, z], dst, qp_sem.at[0]).start()
         send_part(c, 0, matmul(dscores, query, NN))
-        grad_q += matmul(key_cols[:, c * rows : (c + 1) * rows], dscores, NN)
-    grad_q = grad_q.T
-
-    dq_stage[...] = grad_q.astype(jnp.bfloat16).reshape(dq_stage.shape)
-    for w, j in line:
-        dst = dq_out.at[:, columns(my_head)]
-        send(dq_stage.at[core_at[j], z_at[w]], dst, qp_sem.at[my_head], line_id(w, j))
-    own = pltpu.make_async_copy(dq_stage.at[core, z], dq_out.at[:, columns(my_head)], qp_sem.at[my_head])
-    own.start()
-
-    for c in range(chips):
-        for j in range(CORES):
-            for kind in range(2):
-                arrive(parts.at[c, j, kind], p_sem.at[kind, c, j])
-    for h in range(heads):
-        arrive(dq_out.at[:, h * HEAD_DIM : (h + 1) * HEAD_DIM], qp_sem.at[h])
+
     for copy in sent:
         copy.wait_send()
+    arrive(dq_out, qp_sem.at[0])
+    arrive(parts, p_sem.at[0])
 
 
 def sum_kernel(dq, parts, dq_out, dk_out, dv_out, dk_buf, dv_buf, store_sem):
@@ -289,12 +280,12 @@
             pltpu.SMEM(span_place.shape, span_place.dtype),
             dma((copies,)),
             dma((3,)),
-            dma((CORES, head_size)),
-            dma((CORES, head_size)),
-            dma((chips, CORES)),
-            dma((chips, CORES)),
-            dma((2, chips, CORES)),
-            dma((heads,)),
+            dma((1,)),
+            dma((1,)),
+            dma((chips,)),
+            dma((chips,)),
+            dma((1,)),
+            dma((1,)),
         ],
         compiler_params=pltpu.CompilerParams(
             collective_id=0, has_side_effects=True, vmem_limit_bytes=GRANT

time: 22.2 us -> 21.7 us (0.977)
  Pallas kernels: 21.4 us -> 20.9 us
    pallas_call x1, Pallas kernels: 20.7 us -> 20.1 us  [body(): pl.pallas_call(functools.partial(kernel, ctx_size, head_size), out_shape=...]
where the time goes in v10:
time: 21.7 us; the launch traced here: 21.5 us
  Pallas kernels  20.9 us (96%)
  between operations  0.64 us (3%)
    pallas_call x1, Pallas kernels, body(): pl.pallas_call(functools.partial(kernel, ctx_size, head_size), out_shape=...  20.1 us
    pallas_call x1, Pallas kernels, body(): pl.pallas_call(sum_kernel, out_shape=tuple((jax.ShapeDtypeStruct(shape, l...  0.73 us

profile of v10, /device:TPU:0, one launch (start us, length us, event | category | flops | bytes accessed | tf_op | source)
XLA Modules:
  0.0 21.5 jit_solution(13382444783914041581)
XLA Ops:
  0.6 20.1 %shard_map.85 = (bf16[32,1024]{1,0:T(8,128)(2,1)S(1)}, bf16[4,2,2,128,128]{4,3,2,1,0:T(8,128)(2,1)S(1)}) custom-call(s32[16]{0:T(128)} %place_in.1, bf16[32,1024]{1,0:T(8,128)(2,1)} %query_in.1, bf16[128,256]{1,0:T(8,128)(2,1)} %key_in.1, bf16[128,256]{1,0:T(8,128)(2,1)} %value_in.1, bf16[32,1024]{1,0:T(8,128)(2,1)} %saved_in.1, bf16[32,1024]{1,0:T(8,128)(2,1)} %grad_in.1), custom_call_target="tpu_custom_call" | custom-call | flops 335544320 | bytes 327680 | tf_op jit(solution)/shard_map/pallas_call | solution.py:263
  20.8 0.7 %shard_map.86 = (bf16[32,1024]{1,0:T(8,128)(2,1)}, bf16[128,256]{1,0:T(8,128)(2,1)}, bf16[128,256]{1,0:T(8,128)(2,1)}) custom-call(bf16[32,1024]{1,0:T(8,128)(2,1)S(1)} %get-tuple-element.5.dq, bf16[4,2,2,128,128]{4,3,2,1,0:T(8,128)(2,1)S(1)} %get-tuple-element.6.parts), custom_call_target="tpu_custom_call" | custom-call | tf_op jit(solution)/shard_map/pallas_call | solution.py:298

commit v11 on v10

--- a/solution.py
+++ b/solution.py
@@ -61,8 +61,8 @@
     chip_at = [other_chip(step) for step in range(chips)]
     core_at = [other_core(step) for step in range(CORES)]
     z_at = [other_z(step) for step in range(head_size)]
-    plane = [(c, j) for c in range(chips) for j in range(CORES) if c or j]
-    line = [(w, j) for w in range(head_size) for j in range(CORES) if w or j]
+    plane = [(c, j) for c in range(chips) for j in range(CORES) if c or j][::-1]
+    line = [(w, j) for w in range(head_size) for j in range(CORES) if w or j][::-1]
 
     def plane_id(c, j):
         return {"ctx": chip_at[c] * CORES + core_at[j], "head": z}
@@ -71,7 +71,7 @@
         return {"ctx": chip * CORES + core_at[j], "head": z_at[w]}
 
     barrier = pltpu.get_barrier_semaphore()
-    peers = [plane_id(c, j) for c, j in plane] + [line_id(w, j) for w, j in line if w]
+    peers = [line_id(w, j) for w, j in line if w] + [plane_id(c, j) for c, j in plane]
     for peer in peers:
         pl.semaphore_signal(barrier, inc=1, device_id=peer, device_id_type=MESH)
 
@@ -100,7 +100,7 @@
         pltpu.make_async_copy(dst, dst, sem).wait()
 
     def send_plane(src, dst, sem):
-        for c, j in plane[::-1]:
+        for c, j in plane:
             send(src.at[:, columns(core_at[j])], dst.at[chip, core], sem.at[chip], plane_id(c, j))
 
     for w, j in line:
@@ -206,14 +206,12 @@
         send_part(c, 1, matmul(probs.astype(jnp.bfloat16), grad, NN))
 
     grad_q = jnp.zeros((HEAD_DIM, rows), jnp.float32)
-    order = far_first[-1:] + far_first[:-1]
-    last = order[-1]
-    for c in order:
+    for c in far_first:
         arrive(vbuf.at[chip_at[c]], v_sem.at[chip_at[c]])
         dprobs = matmul(chunk(vbuf, c), grad_cols, NN)
         dscores = (pbuf[c] * (dprobs - delta_row) * scale).astype(jnp.bfloat16)
         grad_q += matmul(key_cols[:, c * rows : (c + 1) * rows], dscores, NN)
-        if c == last:
+        if c == 0:
             dq_stage[...] = grad_q.T.astype(jnp.bfloat16).reshape(dq_stage.shape)
             dst = dq_out.at[:, columns(my_head)]
             for w, j in line:

time: 21.7 us -> 21.7 us (level)
  no operation moved by 1% of the time
where the time goes in v11:
time: 21.7 us; the launch traced here: 21.5 us
  Pallas kernels  20.9 us (96%)
  between operations  0.64 us (3%)
    pallas_call x1, Pallas kernels, body(): pl.pallas_call(functools.partial(kernel, ctx_size, head_size), out_shape=...  20.1 us
    pallas_call x1, Pallas kernels, body(): pl.pallas_call(sum_kernel, out_shape=tuple((jax.ShapeDtypeStruct(shape, l...  0.73 us

profile of v11, /device:TPU:0, one launch (start us, length us, event | category | flops | bytes accessed | tf_op | source)
XLA Modules:
  0.0 21.5 jit_solution(13801762194825538959)
XLA Ops:
  0.6 20.1 %shard_map.85 = (bf16[32,1024]{1,0:T(8,128)(2,1)S(1)}, bf16[4,2,2,128,128]{4,3,2,1,0:T(8,128)(2,1)S(1)}) custom-call(s32[16]{0:T(128)} %place_in.1, bf16[32,1024]{1,0:T(8,128)(2,1)} %query_in.1, bf16[128,256]{1,0:T(8,128)(2,1)} %key_in.1, bf16[128,256]{1,0:T(8,128)(2,1)} %value_in.1, bf16[32,1024]{1,0:T(8,128)(2,1)} %saved_in.1, bf16[32,1024]{1,0:T(8,128)(2,1)} %grad_in.1), custom_call_target="tpu_custom_call" | custom-call | flops 335544320 | bytes 327680 | tf_op jit(solution)/shard_map/pallas_call | solution.py:261
  20.8 0.7 %shard_map.86 = (bf16[32,1024]{1,0:T(8,128)(2,1)}, bf16[128,256]{1,0:T(8,128)(2,1)}, bf16[128,256]{1,0:T(8,128)(2,1)}) custom-call(bf16[32,1024]{1,0:T(8,128)(2,1)S(1)} %get-tuple-element.5.dq, bf16[4,2,2,128,128]{4,3,2,1,0:T(8,128)(2,1)S(1)} %get-tuple-element.6.parts), custom_call_target="tpu_custom_call" | custom-call | tf_op jit(solution)/shard_map/pallas_call | solution.py:296

commit v12 on v11

--- a/solution.py
+++ b/solution.py
@@ -203,7 +203,8 @@
     for c in far_first:
         probs = pbuf[c] * weights[c]
         pbuf[c] = probs
-        send_part(c, 1, matmul(probs.astype(jnp.bfloat16), grad, NN))
+        if c:
+            send_part(c, 1, matmul(probs.astype(jnp.bfloat16), grad, NN))
 
     grad_q = jnp.zeros((HEAD_DIM, rows), jnp.float32)
     for c in far_first:
@@ -218,6 +219,7 @@
                 send(dq_stage.at[core_at[j], z_at[w]], dst, qp_sem.at[0], line_id(w, j))
             pltpu.make_async_copy(dq_stage.at[core, z], dst, qp_sem.at[0]).start()
         send_part(c, 0, matmul(dscores, query, NN))
+    send_part(0, 1, matmul(pbuf[0].astype(jnp.bfloat16), grad, NN))
 
     for copy in sent:
         copy.wait_send()

time: 21.7 us -> 21.7 us (level)
  no operation moved by 1% of the time
where the time goes in v12:
time: 21.7 us; the launch traced here: 21.5 us
  Pallas kernels  20.9 us (96%)
  between operations  0.64 us (3%)
    pallas_call x1, Pallas kernels, body(): pl.pallas_call(functools.partial(kernel, ctx_size, head_size), out_shape=...  20.1 us
    pallas_call x1, Pallas kernels, body(): pl.pallas_call(sum_kernel, out_shape=tuple((jax.ShapeDtypeStruct(shape, l...  0.73 us

profile of v12, /device:TPU:0, one launch (start us, length us, event | category | flops | bytes accessed | tf_op | source)
XLA Modules:
  0.0 21.5 jit_solution(12198718857788880053)
XLA Ops:
  0.6 20.1 %shard_map.85 = (bf16[32,1024]{1,0:T(8,128)(2,1)S(1)}, bf16[4,2,2,128,128]{4,3,2,1,0:T(8,128)(2,1)S(1)}) custom-call(s32[16]{0:T(128)} %place_in.1, bf16[32,1024]{1,0:T(8,128)(2,1)} %query_in.1, bf16[128,256]{1,0:T(8,128)(2,1)} %key_in.1, bf16[128,256]{1,0:T(8,128)(2,1)} %value_in.1, bf16[32,1024]{1,0:T(8,128)(2,1)} %saved_in.1, bf16[32,1024]{1,0:T(8,128)(2,1)} %grad_in.1), custom_call_target="tpu_custom_call" | custom-call | flops 335544320 | bytes 327680 | tf_op jit(solution)/shard_map/pallas_call | solution.py:263
  20.8 0.7 %shard_map.86 = (bf16[32,1024]{1,0:T(8,128)(2,1)}, bf16[128,256]{1,0:T(8,128)(2,1)}, bf16[128,256]{1,0:T(8,128)(2,1)}) custom-call(bf16[32,1024]{1,0:T(8,128)(2,1)S(1)} %get-tuple-element.5.dq, bf16[4,2,2,128,128]{4,3,2,1,0:T(8,128)(2,1)S(1)} %get-tuple-element.6.parts), custom_call_target="tpu_custom_call" | custom-call | tf_op jit(solution)/shard_map/pallas_call | solution.py:298
